TPU v7x, 128 devices: a whole 4x4x4 slice. The times are simulated.
128 devices in a mesh: lat: 8 (over x_lo, y), lon: 16 (over x_hi, z, core).
Axes of the slice: x: 4 (x_hi: 2, x_lo: 2; x = x_hi * 2 + x_lo), y: 4, z: 4, core: 2. Of those that a mesh axis runs over, the one named last changes fastest.
Arguments:
- grid_rows: bfloat16 [65536, 512], P(('lat', 'lon')), may hold values from -6 to 6
- dest_owner: int32 [65536, 1], P(('lat', 'lon')), may hold values from 0 to 127; in each aligned block of 512 rows (0 to 511, 512 to 1023, ...) at most 8 rows name the same one
- dest_node: int32 [65536], P(('lat', 'lon')), may hold values from 0 to 127
- node_embed: bfloat16 [16384, 512], P(('lat', 'lon')), may hold values from -6 to 6
- neighbours: int32 [128, 16], P(('lat', 'lon')), may hold values from 0 to 127, as said below
- norm_gain: float32 [512], replicated, may hold values from 0.5 to 1.5
- w_qkv: bfloat16 [512, 1536], replicated, may hold values from -4 to 4
- w_out: bfloat16 [512, 512], replicated, may hold values from -0.25 to 0.25
- cotangent: bfloat16 [16384, 512], P(('lat', 'lon')), may hold values from -6 to 6
Outputs:
- mixed: bfloat16 [16384, 512], P(('lat', 'lon'))
- grad_grid: bfloat16 [65536, 512], P(('lat', 'lon'))
- grad_w_qkv: float32 [512, 1536], replicated
- grad_w_out: float32 [512, 512], replicated
- grad_gain: float32 [512], replicated
Inputs may be any that keep to these rules, and one draw needn't show every extreme that they name: dest_owner names a partition (lat index times 16 plus lon index); the 512 rows of one tile name one partition at most 8 times. `neighbours`: block g lies on partition g. Entry 0 of row b is b itself; every listed block lies on b's partition or on one whose lat index differs by at most 1 and whose lon index differs by at most 1 cyclically over 16. Entries may repeat.
All inputs are finite; a program needn't handle non-finite values.
Results may differ from a plain program's by a relative error of at most 0.017.
Values may be sent and summed in bfloat16 or wider, within the bound.
A program may use at most 128 MiB of HBM per device.

v0:
```python
import jax
import jax.numpy as jnp
from jax import lax
from jax.sharding import PartitionSpec as P

HEADS = 16


EPS = 1e-05


def extended(cells, sides, width):
    for axis, dim in sides:
        count = lax.axis_size(axis)
        head = lax.slice_in_dim(cells, 0, width, axis=dim)
        tail = lax.slice_in_dim(cells, cells.shape[dim] - width, cells.shape[dim], axis=dim)
        cells = jnp.concatenate(
            [
                lax.ppermute(tail, axis, [(i, (i + 1) % count) for i in range(count)]),
                cells,
                lax.ppermute(head, axis, [((i + 1) % count, i) for i in range(count)]),
            ],
            axis=dim,
        )
    return cells


def from_behind(value, axis, by):
    length = lax.axis_size(axis)
    return lax.ppermute(value, axis, [(i, (i + by) % length) for i in range(length)])


def attend_block(query_block, keyval_block):
    block_rows, heads, head_size = query_block.shape
    width = heads * head_size
    keys = keyval_block[:, :width].reshape(-1, heads, head_size)
    values = keyval_block[:, width:].reshape(-1, heads, head_size)
    scores = jnp.einsum(
        "qhd,khd->hqk", query_block, keys, preferred_element_type=jnp.float32
    ) * head_size ** (-0.5)
    highest = jnp.max(scores, -1, keepdims=True)
    weights = jnp.exp(scores - highest)
    total = jnp.sum(weights, -1, keepdims=True)
    probs = weights / total
    probs_low = probs.astype(jnp.bfloat16)
    mixed_heads = jnp.einsum("hqk,khd->qhd", probs_low, values, preferred_element_type=jnp.float32)
    attended = mixed_heads.reshape(block_rows, width).astype(jnp.bfloat16)
    return (attended, probs, probs_low, keys, values, highest[..., 0], total[..., 0])


def local(
    grid_rows, dest_owner, dest_node, node_embed, neighbours, norm_gain, w_qkv, w_out, cotangent
):
    lat_count = lax.axis_size("lat")
    lon_count = lax.axis_size("lon")
    devices = lat_count * lon_count
    grid_count, width = grid_rows.shape
    capacity = 2 * grid_count // devices
    node_count = node_embed.shape[0]
    block_count, listed_count = neighbours.shape
    block_rows = node_count // block_count
    head_size = width // HEADS
    scale = head_size ** (-0.5)
    owners = dest_owner[:, 0]
    picked = owners[:, None] == jnp.arange(devices, dtype=jnp.int32)[None, :]
    ranks = jnp.cumsum(picked.astype(jnp.int32), 0) - 1
    slot_index = jnp.sum(jnp.where(picked, ranks, 0), 1)
    flat_index = owners * capacity + slot_index
    send_rows = jnp.zeros((devices * capacity, width), jnp.bfloat16).at[flat_index].set(grid_rows)
    send_nodes = jnp.full((devices * capacity,), -1, jnp.int32).at[flat_index].set(dest_node)
    arrived_rows, arrived_nodes = (
        lax.all_to_all(
            send_rows.reshape(devices, capacity, width),
            ("lat", "lon"),
            split_axis=0,
            concat_axis=0,
            tiled=True,
        ),
        lax.all_to_all(
            send_nodes.reshape(devices, capacity),
            ("lat", "lon"),
            split_axis=0,
            concat_axis=0,
            tiled=True,
        ),
    )
    arrived_rows = arrived_rows.reshape(devices * capacity, width)
    arrived_nodes = arrived_nodes.reshape(devices * capacity)
    members = arrived_nodes[None, :] == jnp.arange(node_count, dtype=jnp.int32)[:, None]
    member_weights = members.astype(jnp.bfloat16)
    totals = jnp.dot(member_weights, arrived_rows, preferred_element_type=jnp.float32)
    counts = jnp.sum(members.astype(jnp.float32), 1)
    divisor = jnp.maximum(counts, 1.0)[:, None]
    latent = node_embed.astype(jnp.float32) + totals / divisor
    mean_value = jnp.mean(latent, -1, keepdims=True)
    centered = latent - mean_value
    inverse_std = lax.rsqrt(jnp.mean(centered * centered, -1, keepdims=True) + EPS)
    normalized = centered * inverse_std
    normed = (normalized * norm_gain).astype(jnp.bfloat16)
    qkv = jnp.dot(normed, w_qkv, preferred_element_type=jnp.float32).astype(jnp.bfloat16)
    queries = qkv[:, :width].reshape(block_count, block_rows, HEADS, head_size)
    keyvals = qkv[:, width:]
    gathered_kv = extended(keyvals[None, None], (("lat", 0), ("lon", 1)), 1)
    pool = gathered_kv.reshape(9 * block_count, block_rows, 2 * width)
    owner_part = neighbours // block_count
    local_block = neighbours % block_count
    lat_step = owner_part // lon_count - lax.axis_index("lat")
    lon_step = (owner_part % lon_count - lax.axis_index("lon") + lon_count + 1) % lon_count - 1
    pool_index = ((lat_step + 1) * 3 + lon_step + 1) * block_count + local_block

    def forward_block(carried):
        query_block, listed = carried
        return attend_block(query_block, pool[listed].reshape(-1, 2 * width))[0]

    attended = lax.map(forward_block, (queries, pool_index)).reshape(node_count, width)
    projected = jnp.dot(attended, w_out, preferred_element_type=jnp.float32)
    mixed = (latent + projected).astype(jnp.bfloat16)
    contract_rows = (((0,), (0,)), ((), ()))
    contract_cols = (((1,), (1,)), ((), ()))
    out_term = lax.dot_general(
        attended, cotangent, contract_rows, preferred_element_type=jnp.float32
    )
    d_attended = lax.dot_general(
        cotangent, w_out, contract_cols, preferred_element_type=jnp.float32
    ).astype(jnp.bfloat16)
    d_blocks = d_attended.reshape(block_count, block_rows, HEADS, head_size)

    def backward_block(carried):
        query_block, listed, d_block = carried
        unused, probs, probs_low, keys, values, highest, total = attend_block(
            query_block, pool[listed].reshape(-1, 2 * width)
        )
        d_probs = jnp.einsum("qhd,khd->hqk", d_block, values, preferred_element_type=jnp.float32)
        row_product = jnp.sum(probs * d_probs, -1)
        d_scores = (probs * (d_probs - row_product[..., None])).astype(jnp.bfloat16)
        d_query = (
            jnp.einsum("hqk,khd->qhd", d_scores, keys, preferred_element_type=jnp.float32) * scale
        )
        d_keys = (
            jnp.einsum("hqk,qhd->khd", d_scores, query_block, preferred_element_type=jnp.float32)
            * scale
        )
        d_values = jnp.einsum(
            "hqk,qhd->khd", probs_low, d_block, preferred_element_type=jnp.float32
        )
        both = jnp.concatenate([d_keys.reshape(-1, width), d_values.reshape(-1, width)], 1)
        return (d_query.reshape(block_rows, width), both, highest, total, row_product)

    d_queries, d_parts, row_highs, row_totals, row_products = lax.map(
        backward_block, (queries, pool_index, d_blocks)
    )
    pool_grad = (
        jnp.zeros((9 * block_count, block_rows, 2 * width), jnp.float32)
        .at[pool_index.reshape(-1)]
        .add(d_parts.reshape(block_count * listed_count, block_rows, 2 * width))
    )
    pool_grad = pool_grad.reshape(3, 3, node_count, 2 * width)
    band_sum = pool_grad[1]
    for offset in (-1, 1):
        band_sum = band_sum + from_behind(
            pool_grad[1 + offset].astype(jnp.bfloat16), "lat", offset
        ).astype(jnp.float32)
    cell_sum = band_sum[1]
    for offset in (-1, 1):
        cell_sum = cell_sum + from_behind(
            band_sum[1 + offset].astype(jnp.bfloat16), "lon", offset
        ).astype(jnp.float32)
    d_qkv = jnp.concatenate([d_queries.reshape(node_count, width), cell_sum], 1).astype(
        jnp.bfloat16
    )
    qkv_term = lax.dot_general(normed, d_qkv, contract_rows, preferred_element_type=jnp.float32)
    d_normed = lax.dot_general(d_qkv, w_qkv, contract_cols, preferred_element_type=jnp.float32)
    gain_term = jnp.sum(d_normed * normalized, 0)
    grad_w_qkv, grad_w_out, grad_gain = lax.psum((qkv_term, out_term, gain_term), ("lat", "lon"))
    scaled = d_normed * norm_gain
    d_latent = cotangent.astype(jnp.float32) + inverse_std * (
        scaled
        - jnp.mean(scaled, -1, keepdims=True)
        - normalized * jnp.mean(scaled * normalized, -1, keepdims=True)
    )
    node_grad = (d_latent / divisor).astype(jnp.bfloat16)
    slot_grads = lax.dot_general(
        member_weights, node_grad, contract_rows, preferred_element_type=jnp.float32
    ).astype(jnp.bfloat16)
    returned = lax.all_to_all(
        slot_grads.reshape(devices, capacity, width),
        ("lat", "lon"),
        split_axis=0,
        concat_axis=0,
        tiled=True,
    )
    grad_grid = returned.reshape(devices * capacity, width)[flat_index]
    return (mixed, grad_grid, grad_w_qkv, grad_w_out, grad_gain)


def solution(mesh):
    in_specs = (
        P(("lat", "lon"), None),
        P(("lat", "lon"), None),
        P(("lat", "lon")),
        P(("lat", "lon"), None),
        P(("lat", "lon"), None),
        P(),
        P(),
        P(),
        P(("lat", "lon"), None),
    )
    out_specs = (P(("lat", "lon"), None), P(("lat", "lon"), None), P(), P(), P())
    return jax.shard_map(local, mesh=mesh, in_specs=in_specs, out_specs=out_specs, check_vma=False)
```

profile of v0, /device:TPU:1, one launch (start us, length us, event | category | flops | bytes accessed | tf_op | source)
XLA Modules:
  0.0 414.0 jit_solution(13516945082993116809)
XLA Ops:
  13.4 11.5 %all-to-all-start = ((s32[128,1,8]{2,1,0:T(1,128)}), s32[128,1,8]{2,1,0:T(1,128)S(1)}, u32[]{:S(2)}, u32[]{:S(2)}) async-start(s32[128,1,8]{2,1,0:T(1,128)} %bitcast.7), calls=%async_computation | async-start | bytes 131072 | tf_op jit(solution)/shard_map/all_to_all | solution.py:79
  24.9 4.0 scatter_custom_fusion.1
  28.9 5.6 %all-to-all-done = s32[128,1,8]{2,1,0:T(1,128)S(1)} async-done(((s32[128,1,8]{2,1,0:T(1,128)}), s32[128,1,8]{2,1,0:T(1,128)S(1)}, u32[]{:S(2)}, u32[]{:S(2)}) %all-to-all-start) | async-done | bytes 4128 | tf_op jit(solution)/shard_map/all_to_all | solution.py:79
  34.5 5.2 %all-to-all-start.1 = ((bf16[128,8,512]{2,1,0:T(8,128)(2,1)}), bf16[128,8,512]{2,1,0:T(8,128)(2,1)}, u32[]{:S(2)}, u32[]{:S(2)}) async-start(bf16[128,8,512]{2,1,0:T(8,128)(2,1)} %bitcast.8), calls=%async_computation.1 | async-start | bytes 2097152 | tf_op jit(solution)/shard_map/all_to_all | solution.py:72
  41.3 17.4 %all-to-all-done.1 = bf16[128,8,512]{2,1,0:T(8,128)(2,1)} async-done(((bf16[128,8,512]{2,1,0:T(8,128)(2,1)}), bf16[128,8,512]{2,1,0:T(8,128)(2,1)}, u32[]{:S(2)}, u32[]{:S(2)}) %all-to-all-start.1) | async-done | bytes 1048608 | tf_op jit(solution)/shard_map/all_to_all | solution.py:72
  61.2 3.6 collective-permute-start.1
  64.7 6.1 %collective-permute-done = bf16[1,1,128,1024]{3,2,1,0:T(8,128)(2,1)S(1)} collective-permute-done((bf16[1,1,128,1024]{3,2,1,0:T(8,128)(2,1)S(1)}, bf16[1,1,128,1024]{3,2,1,0:T(8,128)(2,1)S(1)}, u32[]{:S(2)}, u32[]{:S(2)}) %collective-permute-start) | collective-permute-done | bytes 262176 | tf_op jit(solution)/shard_map/ppermute | solution.py:19
  76.7 5.9 %collective-permute-done.2 = bf16[3,1,128,1024]{3,2,1,0:T(8,128)(2,1)} collective-permute-done((bf16[3,1,128,1024]{3,2,1,0:T(8,128)(2,1)}, bf16[3,1,128,1024]{3,2,1,0:T(8,128)(2,1)}, u32[]{:S(2)}, u32[]{:S(2)}) %collective-permute-start.2) | collective-permute-done | bytes 786464 | tf_op jit(solution)/shard_map/ppermute | solution.py:19
  88.1 4.5 %gather_fusion = bf16[16,128,1024]{2,1,0:T(8,128)(2,1)} fusion(bf16[9,128,1024]{2,1,0:T(8,128)(2,1)} %bitcast.88, s32[1024]{0:T(1024)} %pad_clamp_fusion.1), kind=kCustom, calls=%fused_computation | custom fusion | bytes 8388672 | tf_op jit(solution)/shard_map/while/body/eval_jaxpr/gather | solution.py:113
  92.7 4.5 %fusion.52 = (bf16[2048,512]{1,0:T(8,128)(2,1)}, bf16[2048,512]{1,0:T(8,128)(2,1)}) fusion(bf16[2048,1024]{1,0:T(8,128)(2,1)} %bitcast.89), kind=kLoop, calls=%fused_computation.103 | loop fusion | bytes 8388608 | tf_op jit(solution)/shard_map/while/body/eval_jaxpr/slice | solution.py:36
  97.2 4.0 copy.52
  101.2 3.9 copy.51
  105.1 9.6 %fusion.55 = (f32[16,128]{1,0:T(8,128)S(1)}, f32[16,128,2048]{2,1,0:T(8,128)}) fusion(bf16[128,16,32]{0,2,1:T(8,128)(2,1)S(1)} %bitcast.97, bf16[2048,16,32]{0,2,1:T(8,128)(2,1)} %bitcast.92), kind=kOutput, calls=%fused_computation.106 | convolution fusion | flops 281020416 | bytes 19013632 | tf_op jit(solution)/shard_map/while/body/eval_jaxpr/sub | solution.py:42
  114.7 9.3 %fusion.5 = f32[16,32,2048]{2,1,0:T(8,128)} fusion(bf16[128,16,32]{0,2,1:T(8,128)(2,1)S(1)} %bitcast.102, f32[16,128,2048]{2,1,0:T(8,128)} %get-tuple-element.57, f32[16,128]{1,0:T(8,128)S(1)} %get-tuple-element.56), kind=kOutput, calls=%fused_computation.14 | convolution fusion | flops 276824064 | bytes 21110784 | tf_op jit(solution)/shard_map/while/body/eval_jaxpr/hqk,qhd->khd/dot_general | solution.py:143
  124.0 10.5 %multiply_reduce_fusion = (f32[16,128]{1,0:T(8,128)S(1)}, f32[16,128,2048]{2,1,0:T(8,128)}) fusion(f32[16,128,2048]{2,1,0:T(8,128)} %get-tuple-element.57, f32[16,128]{1,0:T(8,128)S(1)} %get-tuple-element.56, bf16[128,16,32]{0,2,1:T(8,128)(2,1)S(1)} %bitcast.103, bf16[2048,16,32]{0,2,1:T(8,128)(2,1)S(1)} %bitcast.95), kind=kOutput, calls=%fused_computation.7 | convolution fusion | flops 281016320 | bytes 35799040 | tf_op jit(solution)/shard_map/while/body/eval_jaxpr/qhd,khd->hqk/dot_general | solution.py:133
  134.4 11.4 %multiply_convert_fusion = bf16[16,128,2048]{2,1,0:T(8,128)(2,1)S(1)} fusion(f32[16,128,2048]{2,1,0:T(8,128)} %get-tuple-element.59, f32[16,128]{1,0:T(8,128)S(1)} %get-tuple-element.58, f32[16,128,2048]{2,1,0:T(8,128)} %get-tuple-element.57, f32[16,128]{1,0:T(8,128)S(1)} %get-tuple-element.56), kind=kLoop, calls=%fused_computation.6 | loop fusion | flops 16777216 | bytes 41959424 | tf_op jit(solution)/shard_map/while/body/eval_jaxpr/convert_element_type | solution.py:135
  152.0 5.3 %copy.48 = f32[16,128,512]{2,1,0:T(8,128)} copy(f32[16,128,512]{1,0,2:T(8,128)} %bitcast.90) | data formatting | bytes 8388608 | tf_op jit(solution)/shard_map/while/body/eval_jaxpr/concatenate | solution.py:146
  157.3 5.1 %copy.54 = f32[64,8,16,128]{3,2,1,0:T(8,128)} copy(f32[64,8,16,128]{3,1,2,0:T(8,128)} %bitcast.94) | data formatting | bytes 8388608
  162.4 5.4 %copy.49 = f32[16,128,512]{2,1,0:T(8,128)} copy(f32[16,128,512]{1,0,2:T(8,128)} %bitcast.91) | data formatting | bytes 8388608 | tf_op jit(solution)/shard_map/while/body/eval_jaxpr/concatenate | solution.py:146
  167.8 8.1 %pad_maximum_fusion = f32[16,128,1024]{2,1,0:T(8,128)} fusion(f32[16,128,512]{2,1,0:T(8,128)} %copy.49, f32[16,128,512]{2,1,0:T(8,128)} %copy.48), kind=kLoop, calls=%fused_computation.11 | loop fusion | flops 2097152 | bytes 16777216 | tf_op jit(solution)/shard_map/while/body/eval_jaxpr/concatenate | solution.py:146
  178.7 17.6 %scatter_fusion = f32[9,128,1024]{2,1,0:T(8,128)} fusion(f32[9,128,1024]{2,1,0:T(8,128)} %broadcast_in_dim.39, s32[16]{0:T(128)S(1)} %copy-done.12, f32[16,128,1024]{2,1,0:T(8,128)} %pad_maximum_fusion), kind=kCustom, calls=%fused_computation.4 | custom fusion | flops 2097152 | bytes 25165888 | tf_op jit(solution)/shard_map/scatter-add | solution.py:155
  199.3 3.6 collective-permute-start.4
  203.0 9.0 %fusion.16 = bf16[16,32,128]{2,1,0:T(8,128)(2,1)S(1)} fusion(bf16[2048,16,32]{0,2,1:T(8,128)(2,1)S(1)} %bitcast.96, f32[16,128,2048]{2,1,0:T(8,128)} %get-tuple-element.57, f32[16,128]{1,0:T(8,128)S(1)} %get-tuple-element.56), kind=kOutput, calls=%fused_computation.32 | convolution fusion | flops 276889600 | bytes 19013632 | tf_op jit(solution)/shard_map/while/body/eval_jaxpr/hqk,khd->qhd/dot_general | solution.py:46
  212.0 4.2 %collective-permute-done.4 = bf16[3,128,1024]{2,1,0:T(8,128)(2,1)S(1)} collective-permute-done((bf16[3,128,1024]{2,1,0:T(8,128)(2,1)S(1)}, bf16[3,128,1024]{2,1,0:T(8,128)(2,1)S(1)}, u32[]{:S(2)}, u32[]{:S(2)}) %collective-permute-start.4) | collective-permute-done | bytes 786464 | tf_op jit(solution)/shard_map/ppermute | solution.py:30
  216.1 4.1 collective-permute-done.5
  220.3 3.3 fusion.50
  224.4 4.9 %collective-permute-start.6 = (bf16[128,1024]{1,0:T(8,128)(2,1)}, bf16[128,1024]{1,0:T(8,128)(2,1)S(1)}, u32[]{:S(2)}, u32[]{:S(2)}) collective-permute-start(bf16[128,1024]{1,0:T(8,128)(2,1)} %get-tuple-element.52), channel_id=1, source_target_pairs={{0,15},{1,0},{2,1},{3,2},{4,3},{5,4},{6,5},{7,6},{8,7},{9,8},{10,9... | collective-permute-start | bytes 786440 | tf_op jit(solution)/shard_map/ppermute | solution.py:30
  234.8 3.1 fusion.30
  240.7 10.2 %all-to-all-start.2 = ((bf16[128,8,512]{2,1,0:T(8,128)(2,1)}), bf16[128,8,512]{2,1,0:T(8,128)(2,1)S(1)}, u32[]{:S(2)}, u32[]{:S(2)}) async-start(bf16[128,8,512]{2,1,0:T(8,128)(2,1)} %fusion.12), calls=%async_computation.2 | async-start | bytes 2097152 | tf_op jit(solution)/shard_map/all_to_all | solution.py:185
  251.8 72.3 %psum.23 = f32[512]{0:T(512)} all-reduce(f32[512]{0:T(512)} %get-tuple-element.34), channel_id=1, replica_groups=mesh['lat'=8,'lon'=16] {'lat','lon'}, use_global_device_ids=true, to_apply=%region_17.18 | all-reduce | flops 512 | bytes 4096 | tf_op jit(solution)/shard_map/psum | solution.py:174
  326.7 75.6 %all-reduce.3.cloned.1.call-done = (f32[512,1536]{1,0:T(8,128)}, f32[512,512]{1,0:T(8,128)}) async-done(((f32[512,1536]{1,0:T(8,128)}, f32[512,512]{1,0:T(8,128)}), (f32[512,1536]{1,0:T(8,128)}, f32[512,512]{1,0:T(8,128)})) %all-reduce.3.cloned.1.call-update) | async-done | bytes 4194320 | tf_op jit(solution)/shard_map/psum | solution.py:174
  402.4 3.8 copy.58
  (100 shorter events, 47.1 us)
Async XLA Ops:
  7.2 53.4 %copy-start = (bf16[512,1536]{1,0:T(8,128)(2,1)S(1)}, bf16[512,1536]{1,0:T(8,128)(2,1)}, u32[]{:S(2)}) copy-start(bf16[512,1536]{1,0:T(8,128)(2,1)} %param.15) | copy-start | bytes 4718596
  7.2 51.6 %copy-start.17 = (bf16[128,512]{1,0:T(8,128)(2,1)S(1)}, bf16[128,512]{1,0:T(8,128)(2,1)}, u32[]{:S(2)}) copy-start(bf16[128,512]{1,0:T(8,128)(2,1)} %param.12) | copy-start | bytes 393220
  7.2 53.4 %copy-start.10 = (f32[512]{0:T(512)S(1)}, f32[512]{0:T(512)}, u32[]{:S(2)}) copy-start(f32[512]{0:T(512)} %param.14) | copy-start | bytes 6148
  13.4 21.1 %all-to-all-start = ((s32[128,1,8]{2,1,0:T(1,128)}), s32[128,1,8]{2,1,0:T(1,128)S(1)}, u32[]{:S(2)}, u32[]{:S(2)}) async-start(s32[128,1,8]{2,1,0:T(1,128)} %bitcast.7), calls=%async_computation | async-start | bytes 131072 | tf_op jit(solution)/shard_map/all_to_all | solution.py:79
  34.5 39.2 %copy-start.5 = (bf16[512,512]{1,0:T(8,128)(2,1)S(1)}, bf16[512,512]{1,0:T(8,128)(2,1)}, u32[]{:S(2)}) copy-start(bf16[512,512]{1,0:T(8,128)(2,1)} %param.16) | copy-start | bytes 1572868
  34.5 39.2 %copy-start.6 = (bf16[128,512]{1,0:T(8,128)(2,1)S(1)}, bf16[128,512]{1,0:T(8,128)(2,1)}, u32[]{:S(2)}) copy-start(bf16[128,512]{1,0:T(8,128)(2,1)} %param.17) | copy-start | bytes 393220
  34.5 24.3 %all-to-all-start.1 = ((bf16[128,8,512]{2,1,0:T(8,128)(2,1)}), bf16[128,8,512]{2,1,0:T(8,128)(2,1)}, u32[]{:S(2)}, u32[]{:S(2)}) async-start(bf16[128,8,512]{2,1,0:T(8,128)(2,1)} %bitcast.8), calls=%async_computation.1 | async-start | bytes 2097152 | tf_op jit(solution)/shard_map/all_to_all | solution.py:72
  39.7 362.6 %all-reduce.3.cloned.1.call-start = ((), (), s32[]{:S(2)}) async-start(), calls=%async_computation.3 | async-start | bytes 8388608 | tf_op jit(solution)/shard_map/psum | solution.py:174
  41.3 19.1 %copy-start.15 = (f32[128]{0:T(128)}, f32[128]{0:T(128)S(1)}, u32[]{:S(2)}) copy-start(f32[128]{0:T(128)S(1)} %broadcast_maximum_fusion) | copy-start | bytes 1540
  60.6 13.0 %copy-start.13 = (f32[128]{0:T(128)}, f32[128]{0:T(128)S(1)}, u32[]{:S(2)}) copy-start(f32[128]{0:T(128)S(1)} %add_rsqrt_fusion) | copy-start | bytes 1540
  61.1 9.7 %collective-permute-start = (bf16[1,1,128,1024]{3,2,1,0:T(8,128)(2,1)S(1)}, bf16[1,1,128,1024]{3,2,1,0:T(8,128)(2,1)S(1)}, u32[]{:S(2)}, u32[]{:S(2)}) collective-permute-start(bf16[1,1,128,1024]{3,2,1,0:T(8,128)(2,1)S(1)} %slice_bitcast_fusion.3), channel_id=1, source_target_pairs={{0,16},{16,32},{32,48},{48,64},{64,80},{80,96},{96,112},{112,0},{1... | collective-permute-start | bytes 786440 | tf_op jit(solution)/shard_map/ppermute | solution.py:19
  61.2 9.6 %collective-permute-start.1 = (bf16[1,1,128,1024]{3,2,1,0:T(8,128)(2,1)S(1)}, bf16[1,1,128,1024]{3,2,1,0:T(8,128)(2,1)S(1)}, u32[]{:S(2)}, u32[]{:S(2)}) collective-permute-start(bf16[1,1,128,1024]{3,2,1,0:T(8,128)(2,1)S(1)} %slice_bitcast_fusion.3), channel_id=1, source_target_pairs={{16,0},{32,16},{48,32},{64,48},{80,64},{96,80},{112,96},{0,112},{1... | collective-permute-start | bytes 786440 | tf_op jit(solution)/shard_map/ppermute | solution.py:21
  70.8 0.7 copy-start.8
  72.5 10.2 %collective-permute-start.2 = (bf16[3,1,128,1024]{3,2,1,0:T(8,128)(2,1)}, bf16[3,1,128,1024]{3,2,1,0:T(8,128)(2,1)}, u32[]{:S(2)}, u32[]{:S(2)}) collective-permute-start(bf16[3,1,128,1024]{3,2,1,0:T(8,128)(2,1)} %pad_maximum_fusion.2), channel_id=1, source_target_pairs={{0,1},{1,2},{2,3},{3,4},{4,5},{5,6},{6,7},{7,8},{8,9},{9,10},{10,1... | collective-permute-start | bytes 2359304 | tf_op jit(solution)/shard_map/ppermute | solution.py:19
  73.4 12.0 %collective-permute-start.3 = (bf16[3,1,128,1024]{3,2,1,0:T(8,128)(2,1)}, bf16[3,1,128,1024]{3,2,1,0:T(8,128)(2,1)}, u32[]{:S(2)}, u32[]{:S(2)}) collective-permute-start(bf16[3,1,128,1024]{3,2,1,0:T(8,128)(2,1)} %pad_maximum_fusion.2), channel_id=1, source_target_pairs={{1,0},{2,1},{3,2},{4,3},{5,4},{6,5},{7,6},{8,7},{9,8},{10,9},{11,1... | collective-permute-start | bytes 2359304 | tf_op jit(solution)/shard_map/ppermute | solution.py:21
  75.4 0.5 copy-start.11
  105.1 9.6 %copy-start.9 = (bf16[128,512]{0,1:T(8,128)(2,1)S(1)}, bf16[128,512]{0,1:T(8,128)(2,1)}, u32[]{:S(2)}) copy-start(bf16[128,512]{0,1:T(8,128)(2,1)} %copy.47) | copy-start | bytes 393220
  114.7 9.3 %copy-start.3 = (bf16[2048,512]{0,1:T(8,128)(2,1)S(1)}, bf16[2048,512]{0,1:T(8,128)(2,1)}, u32[]{:S(2)}) copy-start(bf16[2048,512]{0,1:T(8,128)(2,1)} %copy.51) | copy-start | bytes 6291460
  145.9 3.2 copy-start.1
  175.9 2.8 copy-start.12
  196.3 6.7 %copy-start.4 = (bf16[2048,512]{0,1:T(8,128)(2,1)S(1)}, bf16[2048,512]{0,1:T(8,128)(2,1)}, u32[]{:S(2)}) copy-start(bf16[2048,512]{0,1:T(8,128)(2,1)} %copy.51) | copy-start | bytes 6291460
  199.2 30.1 %slice-start = ((s8[8388608]{0:T(1024)(128)(4,1)}), s8[4194304]{0:T(1024)(128)(4,1)S(1)}, s32[]{:S(2)}) async-start(s8[8388608]{0:T(1024)(128)(4,1)} %bitcast.84), calls=%async_computation.4 | async-start | bytes 8388608
  199.3 16.8 %collective-permute-start.4 = (bf16[3,128,1024]{2,1,0:T(8,128)(2,1)S(1)}, bf16[3,128,1024]{2,1,0:T(8,128)(2,1)S(1)}, u32[]{:S(2)}, u32[]{:S(2)}) collective-permute-start(bf16[3,128,1024]{2,1,0:T(8,128)(2,1)S(1)} %get-tuple-element.50), channel_id=1, source_target_pairs={{0,112},{16,0},{32,16},{48,32},{64,48},{80,64},{96,80},{112,96},{1... | collective-permute-start | bytes 2359304 | tf_op jit(solution)/shard_map/ppermute | solution.py:30
  202.9 26.3 %slice-start.1 = ((s8[8388608]{0:T(1024)(128)(4,1)}), s8[4194304]{0:T(1024)(128)(4,1)S(1)}, s32[]{:S(2)}) async-start(s8[8388608]{0:T(1024)(128)(4,1)} %bitcast.84), calls=%async_computation.5 | async-start | bytes 8388608
  203.0 17.3 %collective-permute-start.5 = (bf16[3,128,1024]{2,1,0:T(8,128)(2,1)S(1)}, bf16[3,128,1024]{2,1,0:T(8,128)(2,1)}, u32[]{:S(2)}, u32[]{:S(2)}) collective-permute-start(bf16[3,128,1024]{2,1,0:T(8,128)(2,1)S(1)} %get-tuple-element.51), channel_id=1, source_target_pairs={{0,16},{16,32},{32,48},{48,64},{64,80},{80,96},{96,112},{112,0},{1... | collective-permute-start | bytes 2359304 | tf_op jit(solution)/shard_map/ppermute | solution.py:30
  211.9 17.3 %copy-start.2 = (bf16[2048,512]{0,1:T(8,128)(2,1)S(1)}, bf16[2048,512]{0,1:T(8,128)(2,1)}, u32[]{:S(2)}) copy-start(bf16[2048,512]{0,1:T(8,128)(2,1)} %copy.52) | copy-start | bytes 6291460
  224.4 9.3 %collective-permute-start.6 = (bf16[128,1024]{1,0:T(8,128)(2,1)}, bf16[128,1024]{1,0:T(8,128)(2,1)S(1)}, u32[]{:S(2)}, u32[]{:S(2)}) collective-permute-start(bf16[128,1024]{1,0:T(8,128)(2,1)} %get-tuple-element.52), channel_id=1, source_target_pairs={{0,15},{1,0},{2,1},{3,2},{4,3},{5,4},{6,5},{7,6},{8,7},{9,8},{10,9... | collective-permute-start | bytes 786440 | tf_op jit(solution)/shard_map/ppermute | solution.py:30
  229.2 4.4 %collective-permute-start.7 = (bf16[128,1024]{1,0:T(8,128)(2,1)}, bf16[128,1024]{1,0:T(8,128)(2,1)S(1)}, u32[]{:S(2)}, u32[]{:S(2)}) collective-permute-start(bf16[128,1024]{1,0:T(8,128)(2,1)} %get-tuple-element.53), channel_id=1, source_target_pairs={{0,1},{1,2},{2,3},{3,4},{4,5},{5,6},{6,7},{7,8},{8,9},{9,10},{10,1... | collective-permute-start | bytes 786440 | tf_op jit(solution)/shard_map/ppermute | solution.py:30
  234.8 3.1 copy-start.14
  237.8 1.3 copy-start.16
  240.7 83.4 %all-to-all-start.2 = ((bf16[128,8,512]{2,1,0:T(8,128)(2,1)}), bf16[128,8,512]{2,1,0:T(8,128)(2,1)S(1)}, u32[]{:S(2)}, u32[]{:S(2)}) async-start(bf16[128,8,512]{2,1,0:T(8,128)(2,1)} %fusion.12), calls=%async_computation.2 | async-start | bytes 2097152 | tf_op jit(solution)/shard_map/all_to_all | solution.py:185
  402.4 3.8 copy-start.7
Sparse Core Ops, SparseCore 0:
  238.0 164.3 all-reduce.2
where the time goes:
time: 415 us; the launch traced here: 414 us
  waiting for transfers between devices  122 us (29%)
  blocking collectives  72.3 us (17%)
  local copies, waits for them, and re-layouts  60 us (14%)
  matrix products  52.9 us (13%)
  other arithmetic  52.4 us (13%)
  starting transfers between devices  40.3 us (10%)
  between operations  14.4 us (3%)
    psum x1, waiting for transfers between devices, local(): lax.psum((qkv_term, out_term, gain_term), ('lat', 'lon'))  75.6 us
    psum x1, blocking collectives, local(): lax.psum((qkv_term, out_term, gain_term), ('lat', 'lon'))  72.3 us
    unnamed x46, local copies, waits for them, and re-layouts  24 us
    scatter-add x1, other arithmetic, local(): pool_grad = jnp.zeros((9 * block_count, block_rows, 2 * width), jnp.float...  17.6 us
    all_to_all x1, waiting for transfers between devices, local(): lax.all_to_all(send_rows.reshape(devices, capacity, width), ('lat', 'lon'...  17.4 us
    ppermute x2, waiting for transfers between devices, extended(): lax.ppermute(tail, axis, [(i, (i + 1) % count) for i in range(count)])  12 us
    all_to_all x1, starting transfers between devices, local(): lax.all_to_all(send_nodes.reshape(devices, capacity), ('lat', 'lon'), spl...  11.5 us
    convert_element_type x1, other arithmetic, backward_block(): d_scores = (probs * (d_probs - row_product[..., None])).astype(jnp.bfloat16)  11.4 us
  transfers between devices with their start and end apart: 12, of which 8 were waited for; matrix products, arithmetic and copies ran while one was open for 7% of the time, Pallas kernels for 0%

commit v1 on v0

v1 whole, which is shorter than its diff:
```python
import functools
import math

import jax
import jax.numpy as jnp
from jax import lax
from jax.experimental import pallas as pl
from jax.experimental.pallas import tpu as pltpu
from jax.sharding import PartitionSpec as P

HEADS = 16
HEAD_SIZE = 32
BLOCK = 128
LANES = 128
LAT = 8
LON = 16
DEVICES = LAT * LON
OWN = 4
CAP = 8
EPS = 1e-05
VMEM_LIMIT = 56 * 1024 * 1024
MESH = pl.DeviceIdType.MESH


def dot_rows(a, b):
    return lax.dot_general(a, b, (((0,), (0,)), ((), ())), preferred_element_type=jnp.float32)


def dot_cols(a, b):
    return lax.dot_general(a, b, (((1,), (1,)), ((), ())), preferred_element_type=jnp.float32)


def here():
    return lax.axis_index("lat"), lax.axis_index("lon")


def greet_all(me):
    barrier = pltpu.get_barrier_semaphore()

    def greet(step, carry):
        other = (me + step) % DEVICES
        pl.semaphore_signal(
            barrier, inc=1, device_id=(other // LON, other % LON), device_id_type=MESH
        )
        return carry

    lax.fori_loop(1, DEVICES, greet, 0)
    return barrier


def await_bytes(ref, sem):
    pltpu.make_async_copy(ref, ref, sem).wait()


def send_to(src, dst, send_sem, recv_sem, lat, lon):
    pltpu.make_async_remote_copy(
        src_ref=src,
        dst_ref=dst,
        send_sem=send_sem,
        recv_sem=recv_sem,
        device_id=(lat, lon),
        device_id_type=MESH,
    ).start()


def tile_rows(index, rows):
    return pl.ds(pl.multiple_of(index * rows, rows), rows)


def iota(shape, dim):
    return lax.broadcasted_iota(jnp.int32, shape, dim)


def route_kernel(
    grid_ref, owner_ref, node_ref, embed_ref, gain_ref,
    halo_ref, latent_ref, divisor_ref, spread_ref, flat_ref,
    send, recv, ids_send, ids_recv,
    send_sem, recv_sem, ids_send_sem, ids_recv_sem, halo_send_sem, halo_recv_sem,
):
    f32, bf16 = jnp.float32, jnp.bfloat16
    lat, lon = here()
    me = lat * LON + lon
    barrier = greet_all(me)
    count, width = grid_ref.shape
    nodes = embed_ref.shape[0]
    half = width // 2
    slots = DEVICES * CAP

    owner = owner_ref[...]
    picked = (owner == iota((count, DEVICES), 1)).astype(f32)
    earlier = (iota((count, count), 0) > iota((count, count), 1)).astype(f32).astype(bf16)
    ranks = jnp.dot(earlier, picked.astype(bf16), preferred_element_type=f32)
    slot = jnp.sum(picked * ranks, axis=1, keepdims=True).astype(jnp.int32)
    flat = jnp.broadcast_to(owner * CAP + slot, (count, LANES))
    flat_ref[...] = flat
    flat_row = flat.astype(f32).T[0:1, :].astype(jnp.int32)
    named = (iota((DEVICES, count), 0) == (flat_row >> 3)).astype(f32)
    named = (named * (node_ref[...] + 1).astype(f32)).astype(bf16)
    at_slot = (slot == iota((count, LANES), 1)).astype(f32).astype(bf16)
    ids_send[:, 0, :] = jnp.dot(named, at_slot, preferred_element_type=f32)

    grid = grid_ref[...]
    for k in range(slots // 128):
        chosen = (iota((128, count), 0) + k * 128 == flat_row).astype(f32).astype(bf16)
        block = jnp.dot(chosen, grid, preferred_element_type=f32).reshape(16, CAP, width)
        block = jnp.concatenate([block[:, :, :half], block[:, :, half:]], axis=1)
        send[k * 256:(k + 1) * 256, :] = block.reshape(256, half).astype(bf16)

    pl.semaphore_wait(barrier, DEVICES - 1)

    def push(step, carry):
        other = (me + step) % DEVICES
        send_to(ids_send.at[other], ids_recv.at[me], ids_send_sem, ids_recv_sem, other // LON, other % LON)
        send_to(
            send.at[tile_rows(other, 2 * CAP)], recv.at[tile_rows(me, 2 * CAP)],
            send_sem, recv_sem, other // LON, other % LON,
        )
        return carry

    lax.fori_loop(1, DEVICES, push, 0)
    pltpu.make_async_copy(ids_send.at[me], ids_recv.at[me], ids_recv_sem).start()
    pltpu.make_async_copy(
        send.at[tile_rows(me, 2 * CAP)], recv.at[tile_rows(me, 2 * CAP)], recv_sem
    ).start()

    await_bytes(ids_recv, ids_recv_sem)
    ids = ids_recv[:, 0, :]
    lanes = 2 * slots
    source = (iota((DEVICES, lanes), 0) == (iota((DEVICES, lanes), 1) >> 4)).astype(f32).astype(bf16)
    codes = jnp.dot(ids.T[:CAP, :].astype(bf16), source, preferred_element_type=f32)
    mine = (iota((CAP, lanes), 1) & 7) == iota((CAP, lanes), 0)
    code = jnp.sum(jnp.where(mine, codes, 0.0), axis=0, keepdims=True).astype(jnp.int32)
    which = (iota((1, lanes), 1) >> 3) & 1
    code = jnp.where(code > 0, code - 1 + nodes * which, -1)
    members = (iota((2 * nodes, lanes), 0) == code).astype(f32)
    counts = jnp.sum(members[:nodes, :], axis=1, keepdims=True)
    divisor = jnp.maximum(counts, 1.0)
    divisor_ref[...] = jnp.broadcast_to(divisor, (nodes, LANES))
    members = members.astype(bf16)

    await_bytes(recv, recv_sem)
    sums = jnp.dot(members, recv[...], preferred_element_type=f32)
    totals = jnp.concatenate([sums[:nodes, :], sums[nodes:, :]], axis=1)
    latent = embed_ref[...].astype(f32) + totals / divisor
    latent_ref[...] = latent
    centered = latent - jnp.mean(latent, axis=1, keepdims=True)
    inverse_std = lax.rsqrt(jnp.mean(centered * centered, axis=1, keepdims=True) + EPS)
    own = pl.ds(OWN * BLOCK, BLOCK)
    halo_ref[own, :] = (centered * inverse_std * gain_ref[...]).astype(bf16)
    for c in range(9):
        if c != OWN:
            send_to(
                halo_ref.at[own], halo_ref.at[pl.ds((8 - c) * BLOCK, BLOCK)],
                halo_send_sem, halo_recv_sem,
                (lat + c // 3 - 1 + LAT) % LAT, (lon + c % 3 - 1 + LON) % LON,
            )

    source = (iota((lanes, DEVICES), 1) == (iota((lanes, DEVICES), 0) >> 4)).astype(f32).astype(bf16)
    codes = jnp.dot(source, ids.astype(bf16), preferred_element_type=f32)
    mine = (iota((lanes, LANES), 0) & 7) == iota((lanes, LANES), 1)
    code = jnp.sum(jnp.where(mine, codes, 0.0), axis=1, keepdims=True).astype(jnp.int32)
    which = (iota((lanes, 1), 0) >> 3) & 1
    code = jnp.where(code > 0, code - 1 + nodes * which, -1)
    spread_ref[...] = (iota((lanes, 2 * nodes), 1) == code).astype(f32).astype(bf16)

    await_bytes(ids_send.at[pl.ds(0, DEVICES - 1)], ids_send_sem)
    await_bytes(send.at[pl.ds(0, (DEVICES - 1) * 2 * CAP)], send_sem)
    await_bytes(halo_ref.at[pl.ds(0, 8 * BLOCK)], halo_recv_sem)
    await_bytes(halo_ref.at[pl.ds(0, 8 * BLOCK)], halo_send_sem)


def route(grid_rows, dest_owner, dest_node, node_embed, norm_gain):
    count, width = grid_rows.shape
    nodes = node_embed.shape[0]
    lanes = 2 * DEVICES * CAP
    bf16, f32 = jnp.bfloat16, jnp.float32
    return pl.pallas_call(
        route_kernel,
        name="route",
        out_shape=(
            jax.ShapeDtypeStruct((9 * nodes, width), bf16),
            jax.ShapeDtypeStruct((nodes, width), f32),
            jax.ShapeDtypeStruct((nodes, LANES), f32),
            jax.ShapeDtypeStruct((lanes, 2 * nodes), bf16),
            jax.ShapeDtypeStruct((count, LANES), jnp.int32),
        ),
        in_specs=[pl.BlockSpec(memory_space=pltpu.VMEM)] * 5,
        out_specs=[pl.BlockSpec(memory_space=pltpu.VMEM)] * 5,
        scratch_shapes=[
            pltpu.VMEM((lanes, width // 2), bf16),
            pltpu.VMEM((lanes, width // 2), bf16),
            pltpu.VMEM((DEVICES, 1, LANES), f32),
            pltpu.VMEM((DEVICES, 1, LANES), f32),
        ] + [pltpu.SemaphoreType.DMA] * 6,
        compiler_params=pltpu.CompilerParams(
            collective_id=0, has_side_effects=True, vmem_limit_bytes=VMEM_LIMIT
        ),
    )(grid_rows, dest_owner, dest_node.reshape(1, count), node_embed, norm_gain.reshape(1, width))


def attend_kernel(
    halo_ref, listed_ref, latent_ref, cot_ref, w_qkv_ref, w_out_ref,
    mixed_ref, grads_ref, node_parts_ref,
    keys, values, q_blocks, d_blocks, scores, weights, d_keyvals, attended_t, d_query_t,
):
    f32, bf16 = jnp.float32, jnp.bfloat16
    width = latent_ref.shape[1]
    group_heads = LANES // HEAD_SIZE
    groups = HEADS // group_heads
    columns = group_heads * BLOCK
    scale = HEAD_SIZE ** (-0.5)
    to_log2 = math.log2(math.e)
    lat, lon = lax.axis_index("lat"), lax.axis_index("lon")

    listed = listed_ref[...]
    lat_step = listed // LON - lat
    lon_step = (listed % LON - lon + LON + 1) % LON - 1
    places = (lat_step + 1) * 3 + lon_step + 1
    rows = lax.broadcasted_iota(jnp.int32, (16, listed.shape[1]), 0)
    times = jnp.sum((places == rows).astype(f32), axis=1, keepdims=True)
    bias = jnp.where(times > 0, jnp.log(jnp.maximum(times, 1.0)) * to_log2, -1e30)

    halo = halo_ref[...]
    own = halo_ref[OWN * BLOCK:(OWN + 1) * BLOCK, :]
    keys[...] = jnp.dot(halo, w_qkv_ref[:, width:2 * width], preferred_element_type=f32).astype(bf16)
    values[...] = jnp.dot(halo, w_qkv_ref[:, 2 * width:], preferred_element_type=f32).astype(bf16)
    queries = jnp.dot(own, w_qkv_ref[:, :width], preferred_element_type=f32).astype(bf16)
    cot = cot_ref[...]
    d_attended = dot_cols(cot, w_out_ref[...]).astype(bf16)
    q_t = queries.astype(f32).T.astype(bf16)
    d_t = d_attended.astype(f32).T.astype(bf16)
    q_blocks[...] = jnp.zeros_like(q_blocks)
    d_blocks[...] = jnp.zeros_like(d_blocks)
    for g in range(groups):
        for h in range(group_heads):
            span = slice(h * HEAD_SIZE, (h + 1) * HEAD_SIZE)
            lanes = slice(h * BLOCK, (h + 1) * BLOCK)
            at = g * LANES + h * HEAD_SIZE
            q_blocks[g, span, lanes] = q_t[at:at + HEAD_SIZE, :]
            d_blocks[g, span, lanes] = d_t[at:at + HEAD_SIZE, :]

    def diagonal(full):
        return jnp.concatenate(
            [
                full[h * HEAD_SIZE:(h + 1) * HEAD_SIZE, h * BLOCK:(h + 1) * BLOCK]
                for h in range(group_heads)
            ],
            axis=0,
        )

    def spread(row):
        return jnp.concatenate(
            [
                jnp.broadcast_to(row[:, h * BLOCK:(h + 1) * BLOCK], (HEAD_SIZE, BLOCK))
                for h in range(group_heads)
            ],
            axis=0,
        )

    def group(g, carry):
        lanes = pl.ds(pl.multiple_of(g * LANES, LANES), LANES)
        q_block, d_block = q_blocks[g], d_blocks[g]
        highest = None
        for c in range(9):
            part = slice(c * BLOCK, (c + 1) * BLOCK)
            s = jnp.dot(keys[part, lanes], q_block, preferred_element_type=f32)
            scores[part, :] = s
            top = jnp.max(s, axis=0, keepdims=True) * (scale * to_log2) + bias[c:c + 1, :]
            highest = top if c == 0 else jnp.maximum(highest, top)
        total = jnp.zeros((1, columns), f32)
        for c in range(9):
            part = slice(c * BLOCK, (c + 1) * BLOCK)
            w = jnp.exp2(scores[part, :] * (scale * to_log2) - (highest - bias[c:c + 1, :]))
            total = total + jnp.sum(w, axis=0, keepdims=True)
            weights[part, :] = w.astype(bf16)
        inverse = 1.0 / total
        out_t = dot_rows(values[:, lanes], weights[...])
        out_group = diagonal(out_t) * spread(inverse)
        attended_t[lanes, :] = out_group.astype(bf16)
        d_group = diagonal(d_block.astype(f32))
        product = out_group * d_group
        delta = jnp.concatenate(
            [
                jnp.sum(product[h * HEAD_SIZE:(h + 1) * HEAD_SIZE, :], axis=0, keepdims=True)
                for h in range(group_heads)
            ],
            axis=1,
        )
        d_scaled = (d_block.astype(f32) * inverse).astype(bf16)
        d_keyvals[:, pl.ds(pl.multiple_of(width + g * LANES, LANES), LANES)] = dot_cols(
            weights[...], d_scaled
        ).astype(bf16)
        for c in range(9):
            part = slice(c * BLOCK, (c + 1) * BLOCK)
            d = jnp.dot(values[part, lanes], d_block, preferred_element_type=f32)
            weights[part, :] = (weights[part, :].astype(f32) * (d - delta)).astype(bf16)
        back = inverse * scale
        q_scaled = (q_block.astype(f32) * back).astype(bf16)
        d_keyvals[:, lanes] = dot_cols(weights[...], q_scaled).astype(bf16)
        d_query_t[lanes, :] = (diagonal(dot_rows(keys[:, lanes], weights[...])) * spread(back)).astype(bf16)
        return carry

    lax.fori_loop(0, groups, group, 0)

    attended = attended_t[...].astype(f32).T.astype(bf16)
    d_query = d_query_t[...].astype(f32).T.astype(bf16)
    mixed_ref[...] = (
        latent_ref[...] + jnp.dot(attended, w_out_ref[...], preferred_element_type=f32)
    ).astype(bf16)
    grads_ref[:width, :] = dot_rows(own, d_query).astype(bf16)
    grads_ref[width:2 * width, :] = dot_rows(halo, d_keyvals[:, :width]).astype(bf16)
    grads_ref[2 * width:3 * width, :] = dot_rows(halo, d_keyvals[:, width:]).astype(bf16)
    grads_ref[3 * width:, :] = jnp.dot(
        attended_t[...], cot, preferred_element_type=f32
    ).astype(bf16)
    node_parts_ref[...] = dot_cols(d_keyvals[...], w_qkv_ref[:, width:]).astype(bf16)
    part = slice(OWN * BLOCK, (OWN + 1) * BLOCK)
    node_parts_ref[part, :] = (
        dot_cols(d_keyvals[part, :], w_qkv_ref[:, width:]) + dot_cols(d_query, w_qkv_ref[:, :width])
    ).astype(bf16)


def attend(halo, listed, latent, cotangent, w_qkv, w_out):
    nodes, width = latent.shape
    columns = LANES // HEAD_SIZE * BLOCK
    groups = width // LANES
    pool = halo.shape[0]
    bf16, f32 = jnp.bfloat16, jnp.float32
    return pl.pallas_call(
        attend_kernel,
        name="attend",
        out_shape=(
            jax.ShapeDtypeStruct((nodes, width), bf16),
            jax.ShapeDtypeStruct((4 * width, width), bf16),
            jax.ShapeDtypeStruct((pool, width), bf16),
        ),
        in_specs=[pl.BlockSpec(memory_space=pltpu.VMEM)] * 6,
        out_specs=[pl.BlockSpec(memory_space=pltpu.VMEM)] * 3,
        scratch_shapes=[
            pltpu.VMEM((pool, width), bf16),
            pltpu.VMEM((pool, width), bf16),
            pltpu.VMEM((groups, LANES, columns), bf16),
            pltpu.VMEM((groups, LANES, columns), bf16),
            pltpu.VMEM((pool, columns), f32),
            pltpu.VMEM((pool, columns), bf16),
            pltpu.VMEM((pool, 2 * width), bf16),
            pltpu.VMEM((width, BLOCK), bf16),
            pltpu.VMEM((width, BLOCK), bf16),
        ],
        compiler_params=pltpu.CompilerParams(vmem_limit_bytes=VMEM_LIMIT),
    )(halo, listed, latent, cotangent, w_qkv, w_out)


ORDERS = ("xyz", "yzx", "zxy", "yxz")


def place_on(axis, lat, lon):
    return {"x": (lon // 8) * 2 + lat // 4, "y": lat % 4, "z": (lon // 2) % 4}[axis]


def moved_to(axis, index, lat, lon):
    if axis == "x":
        return (index % 2) * 4 + lat % 4, (index // 2) * 8 + lon % 8
    if axis == "y":
        return (lat // 4) * 4 + index, lon
    return lat, (lon // 8) * 8 + index * 2 + lon % 2


def exchange_kernel(
    grads_ref, parts_ref, latent_ref, divisor_ref, gain_ref, cot_ref, spread_ref,
    reduced_ref, returned_ref,
    from_core, held_0, from_1, held_1, from_2, held_2, from_3, halo, send,
    sum_send_sem, sum_recv_sem, send_sem, recv_sem, halo_send_sem, halo_recv_sem,
):
    f32, bf16 = jnp.float32, jnp.bfloat16
    lat, lon = here()
    me = lat * LON + lon
    barrier = greet_all(me)
    width = latent_ref.shape[1]
    nodes = latent_ref.shape[0]
    half = width // 2
    mats = len(ORDERS)
    core = lon % 2
    core_rows, rows_1, rows_2 = width // 2, width // 8, width // 32
    cols_3 = width // 4
    twin = (lat, lon - core + (1 - core))
    pl.semaphore_wait(barrier, DEVICES - 1)

    for p in range(mats):
        send_to(
            grads_ref.at[pl.ds(pl.multiple_of(p * width + (1 - core) * core_rows, core_rows), core_rows)],
            from_core.at[p], sum_send_sem.at[p, 0], sum_recv_sem.at[p, 0], *twin,
        )
    for c in range(9):
        if c != OWN:
            n = c - (c > OWN)
            send_to(
                parts_ref.at[pl.ds(c * BLOCK, BLOCK)], halo.at[pl.ds(n * BLOCK, BLOCK)],
                halo_send_sem, halo_recv_sem,
                (lat + c // 3 - 1 + LAT) % LAT, (lon + c % 3 - 1 + LON) % LON,
            )

    places = [[place_on(axis, lat, lon) for axis in order] for order in ORDERS]

    def others(p, level):
        axis, i = ORDERS[p][level], places[p][level]
        for k in range(1, 4):
            t = (i + k) % 4
            yield k - 1, t, moved_to(axis, t, lat, lon)

    def start_1(p):
        await_bytes(from_core.at[p], sum_recv_sem.at[p, 0])
        kept = grads_ref[pl.ds(pl.multiple_of(p * width + core * core_rows, core_rows), core_rows), :]
        held_0[p] = (kept.astype(f32) + from_core[p].astype(f32)).astype(bf16)
        for k, t, other in others(p, 0):
            send_to(
                held_0.at[p, tile_rows(t, rows_1)], from_1.at[p, pl.ds(k * rows_1, rows_1)],
                sum_send_sem.at[p, 1], sum_recv_sem.at[p, 1], *other,
            )

    def start_2(p):
        await_bytes(from_1.at[p], sum_recv_sem.at[p, 1])
        total = held_0[p, tile_rows(places[p][0], rows_1), :].astype(f32)
        for k in range(3):
            total = total + from_1[p, k * rows_1:(k + 1) * rows_1, :].astype(f32)
        held_1[p] = total.astype(bf16)
        for k, t, other in others(p, 1):
            send_to(
                held_1.at[p, tile_rows(t, rows_2)], from_2.at[p, pl.ds(k * rows_2, rows_2)],
                sum_send_sem.at[p, 2], sum_recv_sem.at[p, 2], *other,
            )

    def lanes_of(t):
        return pl.ds(pl.multiple_of(t * cols_3, cols_3), cols_3)

    def start_3(p):
        await_bytes(from_2.at[p], sum_recv_sem.at[p, 2])
        total = held_1[p, tile_rows(places[p][1], rows_2), :].astype(f32)
        for k in range(3):
            total = total + from_2[p, k * rows_2:(k + 1) * rows_2, :].astype(f32)
        held_2[p] = total.astype(bf16)
        for k, t, other in others(p, 2):
            send_to(
                held_2.at[p, :, lanes_of(t)], from_3.at[p, pl.ds(k * rows_2, rows_2)],
                sum_send_sem.at[p, 3], sum_recv_sem.at[p, 3], *other,
            )

    def region(p, level):
        row = p * width + core * core_rows
        if level == 0:
            return reduced_ref.at[pl.ds(pl.multiple_of(row, core_rows), core_rows)]
        row = row + places[p][0] * rows_1
        if level == 1:
            return reduced_ref.at[pl.ds(pl.multiple_of(row, rows_1), rows_1)]
        row = row + places[p][1] * rows_2
        return reduced_ref.at[pl.ds(pl.multiple_of(row, rows_2), rows_2)]

    def start_back_3(p):
        await_bytes(from_3.at[p], sum_recv_sem.at[p, 3])
        total = held_2[p, :, lanes_of(places[p][2])].astype(f32)
        for k in range(3):
            total = total + from_3[p, k * rows_2:(k + 1) * rows_2, :].astype(f32)
        piece = region(p, 2).at[:, lanes_of(places[p][2])]
        piece[...] = total.astype(bf16)
        for k, t, other in others(p, 2):
            send_to(piece, piece, sum_send_sem.at[p, 4], sum_recv_sem.at[p, 4], *other)

    def start_back_2(p):
        await_bytes(from_3.at[p], sum_recv_sem.at[p, 4])
        piece = region(p, 2)
        for k, t, other in others(p, 1):
            send_to(piece, piece, sum_send_sem.at[p, 5], sum_recv_sem.at[p, 5], *other)

    def start_back_1(p):
        await_bytes(from_2.at[p], sum_recv_sem.at[p, 5])
        piece = region(p, 1)
        for k, t, other in others(p, 0):
            send_to(piece, piece, sum_send_sem.at[p, 6], sum_recv_sem.at[p, 6], *other)

    def start_back_core(p):
        await_bytes(from_1.at[p], sum_recv_sem.at[p, 6])
        piece = region(p, 0)
        send_to(piece, piece, sum_send_sem.at[p, 7], sum_recv_sem.at[p, 7], *twin)

    for p in range(mats):
        start_1(p)

    await_bytes(halo, halo_recv_sem)
    d_normed = parts_ref[OWN * BLOCK:(OWN + 1) * BLOCK, :].astype(f32)
    for n in range(8):
        d_normed = d_normed + halo[n * BLOCK:(n + 1) * BLOCK, :].astype(f32)
    latent = latent_ref[...]
    centered = latent - jnp.mean(latent, axis=1, keepdims=True)
    inverse_std = lax.rsqrt(jnp.mean(centered * centered, axis=1, keepdims=True) + EPS)
    normalized = centered * inverse_std
    scaled = d_normed * gain_ref[...]
    d_latent = cot_ref[...].astype(f32) + inverse_std * (
        scaled
        - jnp.mean(scaled, axis=1, keepdims=True)
        - normalized * jnp.mean(scaled * normalized, axis=1, keepdims=True)
    )
    node_grad = (d_latent / divisor_ref[:, 0:1]).astype(bf16)
    stacked = jnp.concatenate([node_grad[:, :half], node_grad[:, half:]], axis=0)
    send[...] = jnp.dot(spread_ref[...], stacked, preferred_element_type=f32).astype(bf16)

    def push(step, carry):
        other = (me + step) % DEVICES
        send_to(
            send.at[tile_rows(other, 2 * CAP)], returned_ref.at[tile_rows(me, 2 * CAP)],
            send_sem, recv_sem, other // LON, other % LON,
        )
        return carry

    lax.fori_loop(1, DEVICES, push, 0)
    pltpu.make_async_copy(
        send.at[tile_rows(me, 2 * CAP)], returned_ref.at[tile_rows(me, 2 * CAP)], recv_sem
    ).start()

    for stage in (start_2, start_3, start_back_3, start_back_2, start_back_1, start_back_core):
        for p in range(mats):
            stage(p)
    for p in range(mats):
        await_bytes(from_core.at[p], sum_recv_sem.at[p, 7])
        sizes = (from_core, from_1, from_2, from_3, from_3, from_2, from_1, from_core)
        for level, like in enumerate(sizes):
            await_bytes(like.at[p], sum_send_sem.at[p, level])
    await_bytes(halo, halo_send_sem)
    await_bytes(returned_ref, recv_sem)
    await_bytes(send.at[pl.ds(0, (DEVICES - 1) * 2 * CAP)], send_sem)


def exchange(grads, node_parts, latent, divisor, norm_gain, cotangent, spread):
    nodes, width = latent.shape
    lanes = 2 * DEVICES * CAP
    mats = len(ORDERS)
    bf16 = jnp.bfloat16
    return pl.pallas_call(
        exchange_kernel,
        name="exchange",
        out_shape=(
            jax.ShapeDtypeStruct((4 * width, width), bf16),
            jax.ShapeDtypeStruct((lanes, width // 2), bf16),
        ),
        in_specs=[pl.BlockSpec(memory_space=pltpu.VMEM)] * 7,
        out_specs=[pl.BlockSpec(memory_space=pltpu.VMEM)] * 2,
        scratch_shapes=[
            pltpu.VMEM((mats, width // 2, width), bf16),
            pltpu.VMEM((mats, width // 2, width), bf16),
            pltpu.VMEM((mats, 3 * width // 8, width), bf16),
            pltpu.VMEM((mats, width // 8, width), bf16),
            pltpu.VMEM((mats, 3 * width // 32, width), bf16),
            pltpu.VMEM((mats, width // 32, width), bf16),
            pltpu.VMEM((mats, 3 * width // 32, width // 4), bf16),
            pltpu.VMEM((8 * nodes, width), bf16),
            pltpu.VMEM((lanes, width // 2), bf16),
            pltpu.SemaphoreType.DMA((mats, 8)),
            pltpu.SemaphoreType.DMA((mats, 8)),
        ] + [pltpu.SemaphoreType.DMA] * 4,
        compiler_params=pltpu.CompilerParams(
            collective_id=1, has_side_effects=True, vmem_limit_bytes=VMEM_LIMIT
        ),
    )(grads, node_parts, latent, divisor, norm_gain.reshape(1, width), cotangent, spread)


def finish_kernel(
    reduced_ref, returned_ref, flat_ref, w_qkv_ref, gain_ref,
    grad_grid_ref, grad_w_qkv_ref, grad_w_out_ref, grad_gain_ref,
):
    f32, bf16 = jnp.float32, jnp.bfloat16
    count, width = grad_grid_ref.shape
    half = width // 2
    slots = DEVICES * CAP
    back = returned_ref[...].astype(f32).reshape(DEVICES, 2 * CAP, half)
    back = jnp.concatenate([back[:, :CAP, :], back[:, CAP:, :]], axis=2)
    back = back.reshape(slots, width).astype(bf16)
    chosen = (iota((count, slots), 1) == flat_ref[:, 0:1]).astype(f32).astype(bf16)
    grad_grid_ref[...] = jnp.dot(chosen, back, preferred_element_type=f32).astype(bf16)
    product = jnp.zeros((width, 1), f32)
    for third in range(3):
        span = slice(third * width, (third + 1) * width)
        grad = reduced_ref[span, :].astype(f32)
        grad_w_qkv_ref[:, span] = grad
        product = product + jnp.sum(grad * w_qkv_ref[:, span].astype(f32), axis=1, keepdims=True)
    grad_w_out_ref[...] = reduced_ref[3 * width:, :].astype(f32)
    row = jnp.broadcast_to(product, (width, LANES)).T[0:1, :]
    grad_gain_ref[...] = row / gain_ref[...]


def finish(reduced, returned, flat, w_qkv, norm_gain):
    width = w_qkv.shape[0]
    count = flat.shape[0]
    f32 = jnp.float32
    return pl.pallas_call(
        finish_kernel,
        name="finish",
        out_shape=(
            jax.ShapeDtypeStruct((count, width), jnp.bfloat16),
            jax.ShapeDtypeStruct((width, 3 * width), f32),
            jax.ShapeDtypeStruct((width, width), f32),
            jax.ShapeDtypeStruct((1, width), f32),
        ),
        in_specs=[pl.BlockSpec(memory_space=pltpu.VMEM)] * 5,
        out_specs=[pl.BlockSpec(memory_space=pltpu.VMEM)] * 4,
        compiler_params=pltpu.CompilerParams(vmem_limit_bytes=VMEM_LIMIT),
    )(reduced, returned, flat, w_qkv, norm_gain.reshape(1, width))


def local(
    grid_rows, dest_owner, dest_node, node_embed, neighbours, norm_gain, w_qkv, w_out, cotangent
):
    halo, latent, divisor, spread, flat = route(
        grid_rows, dest_owner, dest_node, node_embed, norm_gain
    )
    mixed, grads, node_parts = attend(halo, neighbours, latent, cotangent, w_qkv, w_out)
    reduced, returned = exchange(
        grads, node_parts, latent, divisor, norm_gain, cotangent, spread
    )
    grad_grid, grad_w_qkv, grad_w_out, grad_gain = finish(reduced, returned, flat, w_qkv, norm_gain)
    return (mixed, grad_grid, grad_w_qkv, grad_w_out, grad_gain.reshape(norm_gain.shape))


def solution(mesh):
    split = P(("lat", "lon"), None)
    in_specs = (split, split, P(("lat", "lon")), split, split, P(), P(), P(), split)
    out_specs = (split, split, P(), P(), P())
    return jax.shard_map(local, mesh=mesh, in_specs=in_specs, out_specs=out_specs, check_vma=False)
```

time: 415 us -> 133 us (0.32)
  Pallas kernels: 0 us -> 131 us
  waiting for transfers between devices: 122 us -> 0 us
  blocking collectives: 72.3 us -> 0 us
  local copies, waits for them, and re-layouts: 60 us -> 1.53 us
  matrix products: 52.9 us -> 0 us
  other arithmetic: 52.4 us -> 0 us
  starting transfers between devices: 40.3 us -> 0 us
  between operations: 14.4 us -> 0.65 us
    pallas_call x0 -> x4, Pallas kernels: none -> 131 us  [the longest x1 62.1 us: exchange(): pl.pallas_call(exchange_kernel, name='exchange', out_shape=(jax.ShapeDtyp...]
    psum x1 -> x0, waiting for transfers between devices: 75.6 us -> none  [local(): lax.psum((qkv_term, out_term, gain_term), ('lat', 'lon'))]
    psum x1 -> x0, blocking collectives: 72.3 us -> none  [local(): lax.psum((qkv_term, out_term, gain_term), ('lat', 'lon'))]
    dot_general x13 -> x0, matrix products: 43.3 us -> none  [the longest x1 10.5 us: backward_block(): jnp.einsum('qhd,khd->hqk', d_block, values, preferred_element_type=jnp.fl...]
    all_to_all x3 -> x0, starting transfers between devices: 26.9 us -> none  [the longest x1 11.5 us: local(): lax.all_to_all(send_nodes.reshape(devices, capacity), ('lat', 'lon'), spl...]
    ppermute x8 -> x0, waiting for transfers between devices: 23.1 us -> none  [the longest x2 12 us: extended(): lax.ppermute(tail, axis, [(i, (i + 1) % count) for i in range(count)])]
    all_to_all x3 -> x0, waiting for transfers between devices: 23 us -> none  [the longest x1 17.4 us: local(): lax.all_to_all(send_rows.reshape(devices, capacity, width), ('lat', 'lon'...]
    unnamed x46 -> x1, local copies, waits for them, and re-layouts: 24 us -> 1.53 us
  transfers between devices with their start and end apart: 12 -> 0, of which waited for: 8 -> 0; matrix products, arithmetic and copies ran while one was open for 7% -> 0% of each run, Pallas kernels for 0% -> 0%
where the time goes in v1:
time: 133 us
  Pallas kernels  131 us (98%)
  local copies, waits for them, and re-layouts  1.53 us (1%)
    pallas_call x1, Pallas kernels, exchange(): pl.pallas_call(exchange_kernel, name='exchange', out_shape=(jax.ShapeDtyp...  62.1 us
    pallas_call x1, Pallas kernels, route(): pl.pallas_call(route_kernel, name='route', out_shape=(jax.ShapeDtypeStruc...  45.6 us
    pallas_call x1, Pallas kernels, attend(): pl.pallas_call(attend_kernel, name='attend', out_shape=(jax.ShapeDtypeStr...  17.7 us
    pallas_call x1, Pallas kernels, finish(): pl.pallas_call(finish_kernel, name='finish', out_shape=(jax.ShapeDtypeStr...  5.19 us

profile of v1, /device:TPU:1, one launch (start us, length us, event | category | flops | bytes accessed | tf_op | source)
XLA Modules:
  0.0 132.8 jit_solution(386247631178494018)
XLA Ops:
  0.6 1.5 %copy.14.owner_ref = s32[512,1]{1,0:T(8,128)} copy(s32[512,1]{0,1:T(1,128)} %param.10) | data formatting | bytes 4096 | tf_op args[1]
  2.2 45.6 %route.1 = (bf16[1152,512]{1,0:T(8,128)(2,1)}, f32[128,512]{1,0:T(8,128)}, f32[128,128]{1,0:T(8,128)}, bf16[2048,256]{1,0:T(8,128)(2,1)}, s32[512,128]{1,0:T(8,128)}) custom-call(bf16[512,512]{1,0:T(8,128)(2,1)} %grid_ref.1, s32[512,1]{1,0:T(8,128)} %copy.14.owner_ref, s32[1,512]{1,0:T(1,128)} %bitcast.6, bf16[128,512]{1,0:T(8,128)(2,1)} %embed_ref.1, ...), custom_call_target="tpu_custom_call" | custom-call | tf_op jit(solution)/shard_map/route/pallas_call | solution.py:177
  47.7 17.7 %attend.1 = (bf16[128,512]{1,0:T(8,128)(2,1)}, bf16[2048,512]{1,0:T(8,128)(2,1)}, bf16[1152,512]{1,0:T(8,128)(2,1)}) custom-call(bf16[1152,512]{1,0:T(8,128)(2,1)} %get-tuple-element.19.halo_ref, s32[1,16]{1,0:T(1,128)} %listed_ref.1, f32[128,512]{1,0:T(8,128)} %get-tuple-element.20.latent_ref, bf16[128,512]{1,0:T(8,128)(2,1)} %cot_ref.3, ...), custom_call_target="tpu_custom_call" | custom-call | tf_op jit(solution)/shard_map/attend/pallas_call | solution.py:329
  65.5 62.1 %exchange.1 = (bf16[2048,512]{1,0:T(8,128)(2,1)}, bf16[2048,256]{1,0:T(8,128)(2,1)}) custom-call(bf16[2048,512]{1,0:T(8,128)(2,1)} %get-tuple-element.22.grads_ref, bf16[1152,512]{1,0:T(8,128)(2,1)} %get-tuple-element.23.parts_ref, f32[128,512]{1,0:T(8,128)} %get-tuple-element.20.latent_ref, f32[128,128]{1,0:T(8,128)} %get-tuple-element.24.divisor_ref, ...), custom_call_target="tpu_custom_call" | custom-call | tf_op jit(solution)/shard_map/exchange/pallas_call | solution.py:537
  127.6 5.2 %finish.1 = (bf16[512,512]{1,0:T(8,128)(2,1)}, f32[512,1536]{1,0:T(8,128)}, f32[512,512]{1,0:T(8,128)}, f32[1,512]{1,0:T(1,128)}) custom-call(bf16[2048,512]{1,0:T(8,128)(2,1)} %get-tuple-element.26.reduced_ref, bf16[2048,256]{1,0:T(8,128)(2,1)} %get-tuple-element.27.returned_ref, s32[512,128]{1,0:T(8,128)} %get-tuple-element.28.flat_ref, ...), custom_call_target="tpu_custom_call" | custom-call | tf_op jit(solution)/shard_map/finish/pallas_call | solution.py:593

commit v2 on v0

v2 whole, which is shorter than its diff:
```python
import math

import jax
import jax.numpy as jnp
from jax import lax
from jax.experimental import pallas as pl
from jax.experimental.pallas import tpu as pltpu
from jax.sharding import PartitionSpec as P

HEADS = 16
HEAD_SIZE = 32
BLOCK = 128
LANES = 128
LAT = 8
LON = 16
DEVICES = LAT * LON
OWN = 4
CAP = 8
GROUPS = 4
GROUP_HEADS = LANES // HEAD_SIZE
COLUMNS = GROUP_HEADS * BLOCK
SCALE = HEAD_SIZE ** (-0.5)
TO_LOG2 = math.log2(math.e)
EPS = 1e-05
VMEM_LIMIT = 56 * 1024 * 1024
MESH = pl.DeviceIdType.MESH
F32, BF16 = jnp.float32, jnp.bfloat16
ORDERS = (
    ("xyz", "yzx", "zxy", "xzy"),
    ("xyz", "yzx", "zxy", "yxz"),
    ("xyz", "yzx", "zxy", "zyx"),
    ("xyz", "yzx", "zxy", "yzx"),
)
ROWS_CORE, ROWS_1, ROWS_2 = 256, 64, 16


def dot(a, b):
    return jnp.dot(a, b, preferred_element_type=F32)


def dot_rows(a, b):
    return lax.dot_general(a, b, (((0,), (0,)), ((), ())), preferred_element_type=F32)


def dot_cols(a, b):
    return lax.dot_general(a, b, (((1,), (1,)), ((), ())), preferred_element_type=F32)


def iota(shape, dim):
    return lax.broadcasted_iota(jnp.int32, shape, dim)


def one_hot(condition):
    return condition.astype(F32).astype(BF16)


def turned(a):
    return a.astype(F32).T.astype(BF16)


def await_bytes(ref, sem):
    pltpu.make_async_copy(ref, ref, sem).wait()


def send_to(src, dst, send_sem, recv_sem, place):
    pltpu.make_async_remote_copy(
        src_ref=src,
        dst_ref=dst,
        send_sem=send_sem,
        recv_sem=recv_sem,
        device_id=place,
        device_id_type=MESH,
    ).start()


def tile_rows(index, rows):
    return pl.ds(pl.multiple_of(index * rows, rows), rows)


def block_rows(c):
    return pl.ds(c * BLOCK, BLOCK)


def around(lat, lon):
    for c in range(9):
        if c != OWN:
            yield c, ((lat + c // 3 - 1 + LAT) % LAT, (lon + c % 3 - 1 + LON) % LON)


def place_on(axis, lat, lon):
    return {"x": (lon // 8) * 2 + lat // 4, "y": lat % 4, "z": (lon // 2) % 4}[axis]


def moved_to(axis, index, lat, lon):
    if axis == "x":
        return (index % 2) * 4 + lat % 4, (index // 2) * 8 + lon % 8
    if axis == "y":
        return (lat // 4) * 4 + index, lon
    return lat, (lon // 8) * 8 + index * 2 + lon % 2


def diagonal(full):
    return jnp.concatenate(
        [
            full[h * HEAD_SIZE:(h + 1) * HEAD_SIZE, h * BLOCK:(h + 1) * BLOCK]
            for h in range(GROUP_HEADS)
        ],
        axis=0,
    )


def spread_heads(row):
    return jnp.concatenate(
        [
            jnp.broadcast_to(row[:, h * BLOCK:(h + 1) * BLOCK], (HEAD_SIZE, BLOCK))
            for h in range(GROUP_HEADS)
        ],
        axis=0,
    )


def sublayer_kernel(
    grid_ref, owner_ref, node_ref, listed_ref, gain_ref, embed_hbm, w_qkv_hbm, w_out_hbm, cot_hbm,
    mixed_ref, reduced_ref, returned_ref, flat_ref,
    embed_ref, w_qkv_ref, w_out_ref, cot_ref,
    send, recv, ids_send, ids_recv,
    halo, halo_t, latent_ref, spread_ref, keys, values, q_blocks, d_blocks,
    scores, weights, inverses, deltas, d_keyvals, attended_t, d_query_t,
    grads, from_core, held_0, from_1, held_1, from_2, from_3, parts, from_around,
    load_sem, send_sem, recv_sem, ids_send_sem, ids_recv_sem, halo_send_sem, halo_recv_sem,
    sum_send_sem, sum_recv_sem, parts_send_sem, parts_recv_sem, back_send_sem, back_recv_sem,
):
    lat, lon = lax.axis_index("lat"), lax.axis_index("lon")
    me = lat * LON + lon
    barrier = pltpu.get_barrier_semaphore()

    def greet(step, carry):
        other = (me + step) % DEVICES
        pl.semaphore_signal(
            barrier, inc=1, device_id=(other // LON, other % LON), device_id_type=MESH
        )
        return carry

    lax.fori_loop(1, DEVICES, greet, 0)
    loads = [
        pltpu.make_async_copy(src, dst, load_sem.at[i])
        for i, (src, dst) in enumerate(
            ((embed_hbm, embed_ref), (w_qkv_hbm, w_qkv_ref), (w_out_hbm, w_out_ref), (cot_hbm, cot_ref))
        )
    ]
    for load in loads:
        load.start()

    count, width = grid_ref.shape
    nodes = embed_ref.shape[0]
    half = width // 2
    slots = DEVICES * CAP

    owner = owner_ref[...]
    picked = (iota((DEVICES, count), 0) == owner).astype(F32)
    earlier = one_hot(iota((count, count), 0) < iota((count, count), 1))
    slot = jnp.sum(picked * dot(picked.astype(BF16), earlier), axis=0, keepdims=True).astype(jnp.int32)
    flat = owner * CAP + slot
    named = (picked * (node_ref[...] + 1).astype(F32)).astype(BF16)
    ids_send[:, 0, :] = dot_cols(named, one_hot(iota((LANES, count), 0) == slot))
    grid = grid_ref[...]

    pl.semaphore_wait(barrier, DEVICES - 1)
    for step in (0, 1, 7, 2, 6, 3, 5, 4):
        to_lat = (lat + step) % LAT
        chosen = one_hot(iota((LON * CAP, count), 0) + to_lat * (LON * CAP) == flat)
        block = dot(chosen, grid).reshape(LON, CAP, width)
        block = jnp.concatenate([block[:, :, :half], block[:, :, half:]], axis=1)
        send[tile_rows(to_lat, 2 * CAP * LON), :] = block.reshape(2 * CAP * LON, half).astype(BF16)

        def push(j, carry, to_lat=to_lat):
            to_lon = (lon + j) % LON
            other = to_lat * LON + to_lon
            send_to(ids_send.at[other], ids_recv.at[me], ids_send_sem, ids_recv_sem, (to_lat, to_lon))
            send_to(
                send.at[tile_rows(other, 2 * CAP)], recv.at[tile_rows(me, 2 * CAP)],
                send_sem, recv_sem, (to_lat, to_lon),
            )
            return carry

        lax.fori_loop(1 if step == 0 else 0, LON, push, 0)
    pltpu.make_async_copy(ids_send.at[me], ids_recv.at[me], ids_recv_sem).start()
    pltpu.make_async_copy(
        send.at[tile_rows(me, 2 * CAP)], recv.at[tile_rows(me, 2 * CAP)], recv_sem
    ).start()

    for load in loads:
        load.wait()
    cot = cot_ref[...]
    d_t = turned(dot_cols(cot, w_out_ref[...]).astype(BF16))
    q_blocks[...] = jnp.zeros_like(q_blocks)
    d_blocks[...] = jnp.zeros_like(d_blocks)

    def blocks_of(target, full_t):
        for g in range(GROUPS):
            for h in range(GROUP_HEADS):
                at = g * LANES + h * HEAD_SIZE
                target[g, h * HEAD_SIZE:(h + 1) * HEAD_SIZE, h * BLOCK:(h + 1) * BLOCK] = full_t[
                    at:at + HEAD_SIZE, :
                ]

    blocks_of(d_blocks, d_t)
    flat_ref[...] = jnp.broadcast_to(flat.astype(F32), (LANES, count)).T.astype(jnp.int32)
    listed = listed_ref[...]
    lat_step = listed // LON - lat
    lon_step = (listed % LON - lon + LON + 1) % LON - 1
    at_place = (lat_step + 1) * 3 + lon_step + 1 == iota((16, listed.shape[1]), 0)
    times = jnp.sum(at_place.astype(F32), axis=1, keepdims=True)
    bias = jnp.where(times > 0, jnp.log(jnp.maximum(times, 1.0)) * TO_LOG2, -1e30)

    await_bytes(ids_recv, ids_recv_sem)
    ids = ids_recv[:, 0, :]
    lanes = 2 * slots
    codes = dot(turned(ids)[:CAP, :], one_hot(iota((DEVICES, lanes), 0) == (iota((DEVICES, lanes), 1) >> 4)))
    mine = (iota((CAP, lanes), 1) & 7) == iota((CAP, lanes), 0)
    code = jnp.sum(jnp.where(mine, codes, 0.0), axis=0, keepdims=True).astype(jnp.int32)
    code = jnp.where(code > 0, code - 1 + nodes * ((iota((1, lanes), 1) >> 3) & 1), -1)
    members = (iota((2 * nodes, lanes), 0) == code).astype(F32)
    divisor = jnp.maximum(jnp.sum(members[:nodes, :], axis=1, keepdims=True), 1.0)
    members = members.astype(BF16)
    await_bytes(recv, recv_sem)
    sums = dot(members, recv[...])
    totals = jnp.concatenate([sums[:nodes, :], sums[nodes:, :]], axis=1)
    latent = embed_ref[...].astype(F32) + totals / divisor
    latent_ref[...] = latent
    centered = latent - jnp.mean(latent, axis=1, keepdims=True)
    inverse_std = lax.rsqrt(jnp.mean(centered * centered, axis=1, keepdims=True) + EPS)
    halo[block_rows(OWN), :] = (centered * inverse_std * gain_ref[...]).astype(BF16)
    for c, place in around(lat, lon):
        send_to(
            halo.at[block_rows(OWN)], halo.at[block_rows(8 - c)], halo_send_sem, halo_recv_sem, place
        )

    own = halo[block_rows(OWN), :]
    own_t = turned(own)
    blocks_of(q_blocks, turned(dot(own, w_qkv_ref[:, :width]).astype(BF16)))

    def project(rows):
        keys[rows, :] = dot(halo[rows, :], w_qkv_ref[:, width:2 * width]).astype(BF16)
        values[rows, :] = dot(halo[rows, :], w_qkv_ref[:, 2 * width:]).astype(BF16)

    project(slice(OWN * BLOCK, (OWN + 1) * BLOCK))
    codes = dot(one_hot(iota((lanes, DEVICES), 1) == (iota((lanes, DEVICES), 0) >> 4)), ids.astype(BF16))
    mine = (iota((lanes, LANES), 0) & 7) == iota((lanes, LANES), 1)
    code = jnp.sum(jnp.where(mine, codes, 0.0), axis=1, keepdims=True).astype(jnp.int32)
    code = jnp.where(code > 0, code - 1 + nodes * ((iota((lanes, 1), 0) >> 3) & 1), -1)
    spread_ref[...] = one_hot(iota((lanes, 2 * nodes), 1) == code)

    await_bytes(halo.at[pl.ds(0, 8 * BLOCK)], halo_recv_sem)
    project(slice(0, OWN * BLOCK))
    project(slice((OWN + 1) * BLOCK, 9 * BLOCK))
    halo_t[...] = turned(halo[...])

    def forward(g, carry):
        cols = pl.ds(pl.multiple_of(g * LANES, LANES), LANES)
        q_block = q_blocks[g]
        highest = None
        for c in range(9):
            part = slice(c * BLOCK, (c + 1) * BLOCK)
            s = dot(keys[part, cols], q_block)
            scores[part, :] = s
            top = jnp.max(s, axis=0, keepdims=True) * (SCALE * TO_LOG2) + bias[c:c + 1, :]
            highest = top if c == 0 else jnp.maximum(highest, top)
        total = jnp.zeros((1, COLUMNS), F32)
        for c in range(9):
            part = slice(c * BLOCK, (c + 1) * BLOCK)
            w = jnp.exp2(scores[part, :] * (SCALE * TO_LOG2) - (highest - bias[c:c + 1, :]))
            total = total + jnp.sum(w, axis=0, keepdims=True)
            weights[g, part, :] = w.astype(BF16)
        inverse = 1.0 / total
        out_group = diagonal(dot_rows(values[:, cols], weights[g])) * spread_heads(inverse)
        attended_t[cols, :] = out_group.astype(BF16)
        product = out_group * diagonal(d_blocks[g].astype(F32))
        delta = jnp.concatenate(
            [
                jnp.sum(product[h * HEAD_SIZE:(h + 1) * HEAD_SIZE, :], axis=0, keepdims=True)
                for h in range(GROUP_HEADS)
            ],
            axis=1,
        )
        inverses[g] = jnp.broadcast_to(inverse, (8, COLUMNS))
        deltas[g] = jnp.broadcast_to(delta, (8, COLUMNS))
        return carry

    lax.fori_loop(0, GROUPS, forward, 0)
    grad_w_out = dot(attended_t[...], cot).astype(BF16)
    for g in range(GROUPS):
        grads[4 * g + 3] = grad_w_out[:, g * LANES:(g + 1) * LANES]

    core = lon % 2
    twin = (lat, lon - core + (1 - core))
    core_rows = tile_rows(core, ROWS_CORE)
    places = {axis: place_on(axis, lat, lon) for axis in "xyz"}

    def group_units(g):
        return pl.ds(4 * g, 4)

    def others(axis):
        for k in range(1, 4):
            t = (places[axis] + k) % 4
            yield k - 1, t, moved_to(axis, t, lat, lon)

    def sum_core(g):
        send_to(
            grads.at[group_units(g), tile_rows(1 - core, ROWS_CORE)], from_core.at[group_units(g)],
            sum_send_sem.at[g, 0], sum_recv_sem.at[g, 0], twin,
        )

    def sum_1(g):
        await_bytes(from_core.at[group_units(g)], sum_recv_sem.at[g, 0])
        for m, order in enumerate(ORDERS[g]):
            u = 4 * g + m
            held_0[u] = (grads[u, core_rows, :].astype(F32) + from_core[u].astype(F32)).astype(BF16)
            for k, t, place in others(order[0]):
                send_to(
                    held_0.at[u, tile_rows(t, ROWS_1)], from_1.at[u, pl.ds(k * ROWS_1, ROWS_1)],
                    sum_send_sem.at[g, 1], sum_recv_sem.at[g, 1], place,
                )

    def sum_2(g):
        await_bytes(from_1.at[group_units(g)], sum_recv_sem.at[g, 1])
        for m, order in enumerate(ORDERS[g]):
            u = 4 * g + m
            total = held_0[u, tile_rows(places[order[0]], ROWS_1), :].astype(F32)
            for k in range(3):
                total = total + from_1[u, k * ROWS_1:(k + 1) * ROWS_1, :].astype(F32)
            held_1[u] = total.astype(BF16)
            for k, t, place in others(order[1]):
                send_to(
                    held_1.at[u, tile_rows(t, ROWS_2)], from_2.at[u, pl.ds(k * ROWS_2, ROWS_2)],
                    sum_send_sem.at[g, 2], sum_recv_sem.at[g, 2], place,
                )

    def sum_3(g):
        await_bytes(from_2.at[group_units(g)], sum_recv_sem.at[g, 2])
        for m, order in enumerate(ORDERS[g]):
            u = 4 * g + m
            total = held_1[u, tile_rows(places[order[1]], ROWS_2), :].astype(F32)
            for k in range(3):
                total = total + from_2[u, k * ROWS_2:(k + 1) * ROWS_2, :].astype(F32)
            mine = from_3.at[u, tile_rows(places[order[2]], ROWS_2)]
            mine[...] = total.astype(BF16)
            for k, t, place in others(order[2]):
                send_to(mine, mine, sum_send_sem.at[g, 3], sum_recv_sem.at[g, 3], place)

    def region(u, order, level):
        row = core * ROWS_CORE + places[order[0]] * ROWS_1
        if level == 1:
            return reduced_ref.at[u, pl.ds(pl.multiple_of(row, ROWS_1), ROWS_1)]
        row = row + places[order[1]] * ROWS_2
        return reduced_ref.at[u, pl.ds(pl.multiple_of(row, ROWS_2), ROWS_2)]

    def back_2(g):
        await_bytes(from_2.at[group_units(g)], sum_recv_sem.at[g, 3])
        for m, order in enumerate(ORDERS[g]):
            u = 4 * g + m
            total = from_3[u, :ROWS_2, :].astype(F32)
            for k in range(1, 4):
                total = total + from_3[u, k * ROWS_2:(k + 1) * ROWS_2, :].astype(F32)
            piece = region(u, order, 2)
            piece[...] = total.astype(BF16)
            for k, t, place in others(order[1]):
                send_to(piece, piece, sum_send_sem.at[g, 4], sum_recv_sem.at[g, 4], place)

    def back_1(g):
        await_bytes(from_2.at[group_units(g)], sum_recv_sem.at[g, 4])
        for m, order in enumerate(ORDERS[g]):
            piece = region(4 * g + m, order, 1)
            for k, t, place in others(order[0]):
                send_to(piece, piece, sum_send_sem.at[g, 5], sum_recv_sem.at[g, 5], place)

    def back_core(g):
        await_bytes(from_1.at[group_units(g)], sum_recv_sem.at[g, 5])
        piece = reduced_ref.at[group_units(g), core_rows]
        send_to(piece, piece, sum_send_sem.at[g, 6], sum_recv_sem.at[g, 6], twin)

    def sum_end(g):
        units = group_units(g)
        await_bytes(from_core.at[units], sum_recv_sem.at[g, 6])
        for level, like in enumerate((from_core, from_1, from_2, from_2, from_2, from_1, from_core)):
            await_bytes(like.at[units], sum_send_sem.at[g, level])

    stages = (sum_core, sum_1, sum_2, sum_3, back_2, back_1, back_core, sum_end)
    reached = [0] * GROUPS

    def advance(*groups):
        for g in groups:
            if reached[g] < len(stages):
                stages[reached[g]](g)
                reached[g] += 1

    for g in range(GROUPS):
        cols = slice(g * LANES, (g + 1) * LANES)
        q_block, d_block = q_blocks[g].astype(F32), d_blocks[g]
        inverse, delta = inverses[g, 0:1, :], deltas[g, 0:1, :]
        d_scaled = (d_block.astype(F32) * inverse).astype(BF16)
        d_values = dot_cols(weights[g], d_scaled).astype(BF16)
        d_keyvals[:, width + g * LANES:width + (g + 1) * LANES] = d_values
        for c in range(9):
            part = slice(c * BLOCK, (c + 1) * BLOCK)
            d = dot(values[part, cols], d_block)
            weights[g, part, :] = (weights[g, part, :].astype(F32) * (d - delta)).astype(BF16)
        back = inverse * SCALE
        d_keys = dot_cols(weights[g], (q_block * back).astype(BF16)).astype(BF16)
        d_keyvals[:, cols] = d_keys
        d_query = (diagonal(dot_rows(keys[:, cols], weights[g])) * spread_heads(back)).astype(BF16)
        d_query_t[cols, :] = d_query
        grads[4 * g] = dot_cols(own_t, d_query).astype(BF16)
        both = dot(halo_t[...], jnp.concatenate([d_keys, d_values], axis=1)).astype(BF16)
        grads[4 * g + 1] = both[:, :LANES]
        grads[4 * g + 2] = both[:, LANES:]
        advance(*range(g + 1))

    for c, place in around(lat, lon):
        parts[block_rows(c), :] = dot_cols(
            d_keyvals[block_rows(c), :], w_qkv_ref[:, width:]
        ).astype(BF16)
        n = c - 1 if c > OWN else c
        send_to(
            parts.at[block_rows(c)], from_around.at[block_rows(n)],
            parts_send_sem, parts_recv_sem, place,
        )
    advance(0, 1, 2, 3)
    d_normed = dot_cols(d_keyvals[block_rows(OWN), :], w_qkv_ref[:, width:]) + dot_cols(
        turned(d_query_t[...]), w_qkv_ref[:, :width]
    )
    mixed_ref[...] = (latent_ref[...] + dot_rows(attended_t[...], w_out_ref[...])).astype(BF16)
    advance(0, 1, 2, 3)
    latent = latent_ref[...]
    centered = latent - jnp.mean(latent, axis=1, keepdims=True)
    inverse_std = lax.rsqrt(jnp.mean(centered * centered, axis=1, keepdims=True) + EPS)
    normalized = centered * inverse_std
    await_bytes(from_around, parts_recv_sem)
    for n in range(8):
        d_normed = d_normed + from_around[block_rows(n), :].astype(F32)
    scaled = d_normed * gain_ref[...]
    d_latent = cot.astype(F32) + inverse_std * (
        scaled
        - jnp.mean(scaled, axis=1, keepdims=True)
        - normalized * jnp.mean(scaled * normalized, axis=1, keepdims=True)
    )
    node_grad = (d_latent / divisor).astype(BF16)
    stacked = jnp.concatenate([node_grad[:, :half], node_grad[:, half:]], axis=0)

    await_bytes(send.at[pl.ds(0, (DEVICES - 1) * 2 * CAP)], send_sem)
    for step in (0, 1, 7, 2, 6, 3, 5, 4):
        to_lat = (lat + step) % LAT
        rows = tile_rows(to_lat, 2 * CAP * LON)
        send[rows, :] = dot(spread_ref[rows, :], stacked).astype(BF16)

        def push_back(j, carry, to_lat=to_lat):
            to_lon = (lon + j) % LON
            other = to_lat * LON + to_lon
            send_to(
                send.at[tile_rows(other, 2 * CAP)], returned_ref.at[tile_rows(me, 2 * CAP)],
                back_send_sem, back_recv_sem, (to_lat, to_lon),
            )
            return carry

        lax.fori_loop(1 if step == 0 else 0, LON, push_back, 0)
    pltpu.make_async_copy(
        send.at[tile_rows(me, 2 * CAP)], returned_ref.at[tile_rows(me, 2 * CAP)], back_recv_sem
    ).start()
    while min(reached) < len(stages):
        advance(0, 1, 2, 3)
    await_bytes(ids_send.at[pl.ds(0, DEVICES - 1)], ids_send_sem)
    await_bytes(halo.at[pl.ds(0, 8 * BLOCK)], halo_send_sem)
    await_bytes(from_around, parts_send_sem)
    await_bytes(send.at[pl.ds(0, (DEVICES - 1) * 2 * CAP)], back_send_sem)
    await_bytes(returned_ref, back_recv_sem)


def sublayer(grid_rows, owner, node, embed, listed, gain, w_qkv, w_out, cotangent):
    count, width = grid_rows.shape
    nodes = embed.shape[0]
    lanes = 2 * DEVICES * CAP
    pool = 9 * nodes
    units = 4 * GROUPS
    vmem, dma = pltpu.VMEM, pltpu.SemaphoreType.DMA
    return pl.pallas_call(
        sublayer_kernel,
        name="sublayer",
        out_shape=(
            jax.ShapeDtypeStruct((nodes, width), BF16),
            jax.ShapeDtypeStruct((units, width, LANES), BF16),
            jax.ShapeDtypeStruct((lanes, width // 2), BF16),
            jax.ShapeDtypeStruct((count, LANES), jnp.int32),
        ),
        in_specs=[pl.BlockSpec(memory_space=vmem)] * 5 + [pl.BlockSpec(memory_space=pl.ANY)] * 4,
        out_specs=[pl.BlockSpec(memory_space=vmem)] * 4,
        scratch_shapes=[
            vmem((nodes, width), BF16),
            vmem(w_qkv.shape, BF16),
            vmem(w_out.shape, BF16),
            vmem((nodes, width), BF16),
            vmem((lanes, width // 2), BF16),
            vmem((lanes, width // 2), BF16),
            vmem((DEVICES, 1, LANES), F32),
            vmem((DEVICES, 1, LANES), F32),
            vmem((pool, width), BF16),
            vmem((width, pool), BF16),
            vmem((nodes, width), F32),
            vmem((lanes, 2 * nodes), BF16),
            vmem((pool, width), BF16),
            vmem((pool, width), BF16),
            vmem((GROUPS, LANES, COLUMNS), BF16),
            vmem((GROUPS, LANES, COLUMNS), BF16),
            vmem((pool, COLUMNS), F32),
            vmem((GROUPS, pool, COLUMNS), BF16),
            vmem((GROUPS, 8, COLUMNS), F32),
            vmem((GROUPS, 8, COLUMNS), F32),
            vmem((pool, 2 * width), BF16),
            vmem((width, BLOCK), BF16),
            vmem((width, BLOCK), BF16),
            vmem((units, width, LANES), BF16),
            vmem((units, ROWS_CORE, LANES), BF16),
            vmem((units, ROWS_CORE, LANES), BF16),
            vmem((units, 3 * ROWS_1, LANES), BF16),
            vmem((units, ROWS_1, LANES), BF16),
            vmem((units, 3 * ROWS_2, LANES), BF16),
            vmem((units, 4 * ROWS_2, LANES), BF16),
            vmem((pool, width), BF16),
            vmem((8 * nodes, width), BF16),
            dma((4,)),
        ] + [dma] * 6 + [dma((GROUPS, 7))] * 2 + [dma] * 4,
        compiler_params=pltpu.CompilerParams(
            collective_id=0, has_side_effects=True, vmem_limit_bytes=VMEM_LIMIT
        ),
    )(
        grid_rows, owner.reshape(1, count), node.reshape(1, count), listed, gain.reshape(1, width),
        embed, w_qkv, w_out, cotangent,
    )


def finish_kernel(
    reduced_ref, returned_ref, flat_ref, w_qkv_ref, gain_ref, mixed_in_ref,
    mixed_ref, grad_grid_ref, grad_w_qkv_ref, grad_w_out_ref, grad_gain_ref,
):
    count, width = grad_grid_ref.shape
    half = width // 2
    slots = DEVICES * CAP
    mixed_ref[...] = mixed_in_ref[...]
    product = jnp.zeros((width, LANES), F32)
    for g in range(GROUPS):
        for m in range(3):
            cols = slice(m * width + g * LANES, m * width + (g + 1) * LANES)
            grad = reduced_ref[4 * g + m].astype(F32)
            grad_w_qkv_ref[:, cols] = grad
            product = product + grad * w_qkv_ref[:, cols].astype(F32)
        grad_w_out_ref[:, g * LANES:(g + 1) * LANES] = reduced_ref[4 * g + 3].astype(F32)
    grad_gain_ref[...] = jnp.sum(product.T, axis=0, keepdims=True) / gain_ref[...]
    back = returned_ref[...].astype(F32).reshape(DEVICES, 2 * CAP, half)
    back = jnp.concatenate([back[:, :CAP, :], back[:, CAP:, :]], axis=2)
    back = back.reshape(slots, width).astype(BF16)
    chosen = one_hot(iota((count, slots), 1) == flat_ref[:, 0:1])
    grad_grid_ref[...] = dot(chosen, back).astype(BF16)


def finish(reduced, returned, flat, w_qkv, gain, mixed):
    width = w_qkv.shape[0]
    count = flat.shape[0]
    return pl.pallas_call(
        finish_kernel,
        name="finish",
        out_shape=(
            jax.ShapeDtypeStruct(mixed.shape, BF16),
            jax.ShapeDtypeStruct((count, width), BF16),
            jax.ShapeDtypeStruct((width, 3 * width), F32),
            jax.ShapeDtypeStruct((width, width), F32),
            jax.ShapeDtypeStruct((1, width), F32),
        ),
        in_specs=[pl.BlockSpec(memory_space=pltpu.VMEM)] * 6,
        out_specs=[pl.BlockSpec(memory_space=pltpu.VMEM)] * 5,
        compiler_params=pltpu.CompilerParams(vmem_limit_bytes=VMEM_LIMIT),
    )(reduced, returned, flat, w_qkv, gain.reshape(1, width), mixed)


def local(
    grid_rows, dest_owner, dest_node, node_embed, neighbours, norm_gain, w_qkv, w_out, cotangent
):
    mixed, reduced, returned, flat = sublayer(
        grid_rows, dest_owner, dest_node, node_embed, neighbours, norm_gain, w_qkv, w_out, cotangent
    )
    mixed, grad_grid, grad_w_qkv, grad_w_out, grad_gain = finish(
        reduced, returned, flat, w_qkv, norm_gain, mixed
    )
    return (mixed, grad_grid, grad_w_qkv, grad_w_out, grad_gain.reshape(norm_gain.shape))


def solution(mesh):
    split = P(("lat", "lon"), None)
    in_specs = (split, split, P(("lat", "lon")), split, split, P(), P(), P(), split)
    out_specs = (split, split, P(), P(), P())
    return jax.shard_map(local, mesh=mesh, in_specs=in_specs, out_specs=out_specs, check_vma=False)
```

time: 415 us -> 119 us (0.29)
  waiting for transfers between devices: 122 us -> 0 us
  Pallas kernels: 0 us -> 118 us
  blocking collectives: 72.3 us -> 0 us
  local copies, waits for them, and re-layouts: 60 us -> 0 us
  matrix products: 52.9 us -> 0 us
  other arithmetic: 52.4 us -> 0 us
  starting transfers between devices: 40.3 us -> 0 us
  between operations: 14.4 us -> 0.64 us
    pallas_call x0 -> x2, Pallas kernels: none -> 118 us  [the longest x1 112 us: sublayer(): pl.pallas_call(sublayer_kernel, name='sublayer', out_shape=(jax.ShapeDtyp...]
    psum x1 -> x0, waiting for transfers between devices: 75.6 us -> none  [local(): lax.psum((qkv_term, out_term, gain_term), ('lat', 'lon'))]
    psum x1 -> x0, blocking collectives: 72.3 us -> none  [local(): lax.psum((qkv_term, out_term, gain_term), ('lat', 'lon'))]
    dot_general x13 -> x0, matrix products: 43.3 us -> none  [the longest x1 10.5 us: backward_block(): jnp.einsum('qhd,khd->hqk', d_block, values, preferred_element_type=jnp.fl...]
    all_to_all x3 -> x0, starting transfers between devices: 26.9 us -> none  [the longest x1 11.5 us: local(): lax.all_to_all(send_nodes.reshape(devices, capacity), ('lat', 'lon'), spl...]
    unnamed x46 -> x0, local copies, waits for them, and re-layouts: 24 us -> none
    ppermute x8 -> x0, waiting for transfers between devices: 23.1 us -> none  [the longest x2 12 us: extended(): lax.ppermute(tail, axis, [(i, (i + 1) % count) for i in range(count)])]
    all_to_all x3 -> x0, waiting for transfers between devices: 23 us -> none  [the longest x1 17.4 us: local(): lax.all_to_all(send_rows.reshape(devices, capacity, width), ('lat', 'lon'...]
  transfers between devices with their start and end apart: 12 -> 0, of which waited for: 8 -> 0; matrix products, arithmetic and copies ran while one was open for 7% -> 0% of each run, Pallas kernels for 0% -> 0%
where the time goes in v2:
time: 119 us
  Pallas kernels  118 us (99%)
    pallas_call x1, Pallas kernels, sublayer(): pl.pallas_call(sublayer_kernel, name='sublayer', out_shape=(jax.ShapeDtyp...  112 us
    pallas_call x1, Pallas kernels, finish(): pl.pallas_call(finish_kernel, name='finish', out_shape=(jax.ShapeDtypeStr...  5.7 us

profile of v2, /device:TPU:1, one launch (start us, length us, event | category | flops | bytes accessed | tf_op | source)
XLA Modules:
  0.0 118.8 jit_solution(3558500775398421538)
XLA Ops:
  0.6 112.5 %sublayer.1 = (bf16[128,512]{1,0:T(8,128)(2,1)}, bf16[16,512,128]{2,1,0:T(8,128)(2,1)}, bf16[2048,256]{1,0:T(8,128)(2,1)}, s32[512,128]{1,0:T(8,128)}) custom-call(bf16[512,512]{1,0:T(8,128)(2,1)} %grid_ref.1, s32[1,512]{1,0:T(1,128)} %bitcast.6, s32[1,512]{1,0:T(1,128)} %bitcast.7, s32[1,16]{1,0:T(1,128)} %listed_ref.1, f32[1,512]{1,0:T(1,128)} %bitcast.4, ...), custom_call_target="tpu_custom_call" | custom-call | tf_op jit(solution)/shard_map/sublayer/pallas_call | solution.py:485
  113.1 5.7 %finish.1 = (bf16[128,512]{1,0:T(8,128)(2,1)}, bf16[512,512]{1,0:T(8,128)(2,1)}, f32[512,1536]{1,0:T(8,128)}, f32[512,512]{1,0:T(8,128)}, f32[1,512]{1,0:T(1,128)}) custom-call(bf16[16,512,128]{2,1,0:T(8,128)(2,1)} %get-tuple-element.14.reduced_ref, bf16[2048,256]{1,0:T(8,128)(2,1)} %get-tuple-element.15.returned_ref, ...), custom_call_target="tpu_custom_call" | custom-call | tf_op jit(solution)/shard_map/finish/pallas_call | solution.py:567

commit v3 on v2

--- a/solution.py
+++ b/solution.py
@@ -25,12 +25,8 @@
 VMEM_LIMIT = 56 * 1024 * 1024
 MESH = pl.DeviceIdType.MESH
 F32, BF16 = jnp.float32, jnp.bfloat16
-ORDERS = (
-    ("xyz", "yzx", "zxy", "xzy"),
-    ("xyz", "yzx", "zxy", "yxz"),
-    ("xyz", "yzx", "zxy", "zyx"),
-    ("xyz", "yzx", "zxy", "yzx"),
-)
+FIRST_AXES = "xyz"
+CHIPS = DEVICES // 2
 ROWS_CORE, ROWS_1, ROWS_2 = 256, 64, 16
 
 
@@ -81,10 +77,18 @@
     return pl.ds(c * BLOCK, BLOCK)
 
 
-def around(lat, lon):
-    for c in range(9):
-        if c != OWN:
-            yield c, ((lat + c // 3 - 1 + LAT) % LAT, (lon + c % 3 - 1 + LON) % LON)
+def beside(lat, lon):
+    for sign in (-1, 1):
+        yield sign, (lat, (lon + sign + LON) % LON)
+
+
+def above(lat, lon):
+    for sign in (-1, 1):
+        yield sign, ((lat + sign + LAT) % LAT, lon)
+
+
+def cell(lat_step, lon_step):
+    return (lat_step + 1) * 3 + lon_step + 1
 
 
 def place_on(axis, lat, lon):
@@ -126,7 +130,7 @@
     send, recv, ids_send, ids_recv,
     halo, halo_t, latent_ref, spread_ref, keys, values, q_blocks, d_blocks,
     scores, weights, inverses, deltas, d_keyvals, attended_t, d_query_t,
-    grads, from_core, held_0, from_1, held_1, from_2, from_3, parts, from_around,
+    grads, from_core, held_0, from_1, held_1, from_plane, from_chips, parts, from_around,
     load_sem, send_sem, recv_sem, ids_send_sem, ids_recv_sem, halo_send_sem, halo_recv_sem,
     sum_send_sem, sum_recv_sem, parts_send_sem, parts_recv_sem, back_send_sem, back_recv_sem,
 ):
@@ -231,10 +235,13 @@
     centered = latent - jnp.mean(latent, axis=1, keepdims=True)
     inverse_std = lax.rsqrt(jnp.mean(centered * centered, axis=1, keepdims=True) + EPS)
     halo[block_rows(OWN), :] = (centered * inverse_std * gain_ref[...]).astype(BF16)
-    for c, place in around(lat, lon):
+    mine = halo.at[block_rows(OWN)]
+    for n, (sign, place) in enumerate(above(lat, lon)):
         send_to(
-            halo.at[block_rows(OWN)], halo.at[block_rows(8 - c)], halo_send_sem, halo_recv_sem, place
+            mine, halo.at[block_rows(cell(-sign, 0))], halo_send_sem.at[n], halo_recv_sem.at[n], place
         )
+    for sign, place in beside(lat, lon):
+        send_to(mine, halo.at[block_rows(cell(0, -sign))], halo_send_sem.at[2], halo_recv_sem.at[2], place)
 
     own = halo[block_rows(OWN), :]
     own_t = turned(own)
@@ -244,6 +251,14 @@
         keys[rows, :] = dot(halo[rows, :], w_qkv_ref[:, width:2 * width]).astype(BF16)
         values[rows, :] = dot(halo[rows, :], w_qkv_ref[:, 2 * width:]).astype(BF16)
 
+    for n, (step, _) in enumerate(above(lat, lon)):
+        block = halo.at[block_rows(cell(-step, 0))]
+        await_bytes(block, halo_recv_sem.at[n])
+        for sign, place in beside(lat, lon):
+            send_to(
+                block, halo.at[block_rows(cell(-step, -sign))],
+                halo_send_sem.at[2], halo_recv_sem.at[2], place,
+            )
     project(slice(OWN * BLOCK, (OWN + 1) * BLOCK))
     codes = dot(one_hot(iota((lanes, DEVICES), 1) == (iota((lanes, DEVICES), 0) >> 4)), ids.astype(BF16))
     mine = (iota((lanes, LANES), 0) & 7) == iota((lanes, LANES), 1)
@@ -251,7 +266,7 @@
     code = jnp.where(code > 0, code - 1 + nodes * ((iota((lanes, 1), 0) >> 3) & 1), -1)
     spread_ref[...] = one_hot(iota((lanes, 2 * nodes), 1) == code)
 
-    await_bytes(halo.at[pl.ds(0, 8 * BLOCK)], halo_recv_sem)
+    await_bytes(halo.at[pl.ds(0, 6 * BLOCK)], halo_recv_sem.at[2])
     project(slice(0, OWN * BLOCK))
     project(slice((OWN + 1) * BLOCK, 9 * BLOCK))
     halo_t[...] = turned(halo[...])
@@ -311,88 +326,135 @@
             sum_send_sem.at[g, 0], sum_recv_sem.at[g, 0], twin,
         )
 
+    def add_core(g):
+        units = group_units(g)
+        await_bytes(from_core.at[units], sum_recv_sem.at[g, 0])
+        held_0[units] = (grads[units, core_rows, :].astype(F32) + from_core[units].astype(F32)).astype(BF16)
+
     def sum_1(g):
-        await_bytes(from_core.at[group_units(g)], sum_recv_sem.at[g, 0])
-        for m, order in enumerate(ORDERS[g]):
-            u = 4 * g + m
-            held_0[u] = (grads[u, core_rows, :].astype(F32) + from_core[u].astype(F32)).astype(BF16)
-            for k, t, place in others(order[0]):
-                send_to(
-                    held_0.at[u, tile_rows(t, ROWS_1)], from_1.at[u, pl.ds(k * ROWS_1, ROWS_1)],
-                    sum_send_sem.at[g, 1], sum_recv_sem.at[g, 1], place,
-                )
-
-    def sum_2(g):
-        await_bytes(from_1.at[group_units(g)], sum_recv_sem.at[g, 1])
-        for m, order in enumerate(ORDERS[g]):
-            u = 4 * g + m
-            total = held_0[u, tile_rows(places[order[0]], ROWS_1), :].astype(F32)
-            for k in range(3):
-                total = total + from_1[u, k * ROWS_1:(k + 1) * ROWS_1, :].astype(F32)
-            held_1[u] = total.astype(BF16)
-            for k, t, place in others(order[1]):
-                send_to(
-                    held_1.at[u, tile_rows(t, ROWS_2)], from_2.at[u, pl.ds(k * ROWS_2, ROWS_2)],
-                    sum_send_sem.at[g, 2], sum_recv_sem.at[g, 2], place,
-                )
-
-    def sum_3(g):
-        await_bytes(from_2.at[group_units(g)], sum_recv_sem.at[g, 2])
-        for m, order in enumerate(ORDERS[g]):
-            u = 4 * g + m
-            total = held_1[u, tile_rows(places[order[1]], ROWS_2), :].astype(F32)
-            for k in range(3):
-                total = total + from_2[u, k * ROWS_2:(k + 1) * ROWS_2, :].astype(F32)
-            mine = from_3.at[u, tile_rows(places[order[2]], ROWS_2)]
-            mine[...] = total.astype(BF16)
-            for k, t, place in others(order[2]):
-                send_to(mine, mine, sum_send_sem.at[g, 3], sum_recv_sem.at[g, 3], place)
-
-    def region(u, order, level):
-        row = core * ROWS_CORE + places[order[0]] * ROWS_1
-        if level == 1:
-            return reduced_ref.at[u, pl.ds(pl.multiple_of(row, ROWS_1), ROWS_1)]
-        row = row + places[order[1]] * ROWS_2
-        return reduced_ref.at[u, pl.ds(pl.multiple_of(row, ROWS_2), ROWS_2)]
-
-    def back_2(g):
-        await_bytes(from_2.at[group_units(g)], sum_recv_sem.at[g, 3])
-        for m, order in enumerate(ORDERS[g]):
-            u = 4 * g + m
-            total = from_3[u, :ROWS_2, :].astype(F32)
-            for k in range(1, 4):
-                total = total + from_3[u, k * ROWS_2:(k + 1) * ROWS_2, :].astype(F32)
-            piece = region(u, order, 2)
-            piece[...] = total.astype(BF16)
-            for k, t, place in others(order[1]):
-                send_to(piece, piece, sum_send_sem.at[g, 4], sum_recv_sem.at[g, 4], place)
+        add_core(g)
+        units = group_units(g)
+        for k, t, place in others(FIRST_AXES[g]):
+            send_to(
+                held_0.at[units, tile_rows(t, ROWS_1)], from_1.at[units, pl.ds(k * ROWS_1, ROWS_1)],
+                sum_send_sem.at[g, 1], sum_recv_sem.at[g, 1], place,
+            )
+
+    def plane_index(g):
+        b, c = (axis for axis in "xyz" if axis != FIRST_AXES[g])
+        return places[b] * 4 + places[c]
+
+    def plane_place(g, j):
+        b, c = (axis for axis in "xyz" if axis != FIRST_AXES[g])
+        return moved_to(c, j % 4, *moved_to(b, j // 4, lat, lon))
+
+    def sum_plane(g):
+        units = group_units(g)
+        await_bytes(from_1.at[units], sum_recv_sem.at[g, 1])
+        total = held_0[units, tile_rows(places[FIRST_AXES[g]], ROWS_1), :].astype(F32)
+        for k in range(3):
+            total = total + from_1[units, pl.ds(k * ROWS_1, ROWS_1), :].astype(F32)
+        held_1[units] = total.astype(BF16)
+        mine = plane_index(g)
+
+        def push_piece(k, carry):
+            j = (mine + k) % 16
+            send_to(
+                held_1.at[4 * g + j // 4, tile_rows(j % 4, ROWS_2)], from_plane.at[g, mine],
+                sum_send_sem.at[g, 2], sum_recv_sem.at[g, 2], plane_place(g, j),
+            )
+            return carry
+
+        lax.fori_loop(1, 16, push_piece, 0)
+        from_plane[g, mine] = held_1[4 * g + mine // 4, tile_rows(mine % 4, ROWS_2), :]
+
+    def back_plane(g):
+        await_bytes(from_plane.at[g, pl.ds(0, 15)], sum_recv_sem.at[g, 2])
+        mine = plane_index(g)
+        row = core * ROWS_CORE + places[FIRST_AXES[g]] * ROWS_1 + (mine % 4) * ROWS_2
+        piece = reduced_ref.at[4 * g + mine // 4, pl.ds(pl.multiple_of(row, ROWS_2), ROWS_2)]
+        piece[...] = jnp.sum(from_plane[g].astype(F32), axis=0).astype(BF16)
+
+        def push_sum(k, carry):
+            send_to(
+                piece, piece, sum_send_sem.at[g, 3], sum_recv_sem.at[g, 3],
+                plane_place(g, (mine + k) % 16),
+            )
+            return carry
+
+        lax.fori_loop(1, 16, push_sum, 0)
 
     def back_1(g):
-        await_bytes(from_2.at[group_units(g)], sum_recv_sem.at[g, 4])
-        for m, order in enumerate(ORDERS[g]):
-            piece = region(4 * g + m, order, 1)
-            for k, t, place in others(order[0]):
-                send_to(piece, piece, sum_send_sem.at[g, 5], sum_recv_sem.at[g, 5], place)
+        await_bytes(from_plane.at[g, pl.ds(0, 15)], sum_recv_sem.at[g, 3])
+        row = core * ROWS_CORE + places[FIRST_AXES[g]] * ROWS_1
+        piece = reduced_ref.at[group_units(g), pl.ds(pl.multiple_of(row, ROWS_1), ROWS_1)]
+        for k, t, place in others(FIRST_AXES[g]):
+            send_to(piece, piece, sum_send_sem.at[g, 4], sum_recv_sem.at[g, 4], place)
 
     def back_core(g):
-        await_bytes(from_1.at[group_units(g)], sum_recv_sem.at[g, 5])
+        await_bytes(from_1.at[group_units(g)], sum_recv_sem.at[g, 4])
         piece = reduced_ref.at[group_units(g), core_rows]
-        send_to(piece, piece, sum_send_sem.at[g, 6], sum_recv_sem.at[g, 6], twin)
+        send_to(piece, piece, sum_send_sem.at[g, 5], sum_recv_sem.at[g, 5], twin)
+
+    chip = places["x"] * 16 + places["y"] * 4 + places["z"]
+
+    def place_of(i):
+        x, y, z = i // 16, (i // 4) % 4, i % 4
+        return (x % 2) * 4 + y, (x // 2) * 8 + z * 2 + core
+
+    def piece_of(i):
+        return i // 16, tile_rows(i % 16, ROWS_2)
+
+    def scatter(g):
+        add_core(g)
+
+        def push_piece(k, carry):
+            i = (chip + k) % CHIPS
+            unit, rows = piece_of(i)
+            send_to(
+                held_0.at[4 * g + unit, rows], from_chips.at[chip],
+                sum_send_sem.at[g, 1], sum_recv_sem.at[g, 1], place_of(i),
+            )
+            return carry
+
+        lax.fori_loop(1, CHIPS, push_piece, 0)
+        unit, rows = piece_of(chip)
+        from_chips[chip] = held_0[4 * g + unit, rows, :]
+
+    def gather(g):
+        await_bytes(from_chips.at[pl.ds(0, CHIPS - 1)], sum_recv_sem.at[g, 1])
+        total = jnp.sum(from_chips[...].astype(F32), axis=0)
+        unit, rows = piece_of(chip)
+        row = core * ROWS_CORE + (chip % 16) * ROWS_2
+        piece = reduced_ref.at[4 * g + unit, pl.ds(pl.multiple_of(row, ROWS_2), ROWS_2)]
+        piece[...] = total.astype(BF16)
+
+        def push_sum(k, carry):
+            send_to(
+                piece, piece, sum_send_sem.at[g, 2], sum_recv_sem.at[g, 2], place_of((chip + k) % CHIPS)
+            )
+            return carry
+
+        lax.fori_loop(1, CHIPS, push_sum, 0)
+
+    def gather_core(g):
+        await_bytes(from_chips.at[pl.ds(0, CHIPS - 1)], sum_recv_sem.at[g, 2])
+        piece = reduced_ref.at[group_units(g), core_rows]
+        send_to(piece, piece, sum_send_sem.at[g, 5], sum_recv_sem.at[g, 5], twin)
 
     def sum_end(g):
         units = group_units(g)
-        await_bytes(from_core.at[units], sum_recv_sem.at[g, 6])
-        for level, like in enumerate((from_core, from_1, from_2, from_2, from_2, from_1, from_core)):
-            await_bytes(like.at[units], sum_send_sem.at[g, level])
-
-    stages = (sum_core, sum_1, sum_2, sum_3, back_2, back_1, back_core, sum_end)
-    reached = [0] * GROUPS
-
-    def advance(*groups):
-        for g in groups:
-            if reached[g] < len(stages):
-                stages[reached[g]](g)
-                reached[g] += 1
+        await_bytes(from_core.at[units], sum_recv_sem.at[g, 5])
+        await_bytes(from_core.at[units], sum_send_sem.at[g, 0])
+        await_bytes(from_core.at[units], sum_send_sem.at[g, 5])
+        if g < len(FIRST_AXES):
+            await_bytes(from_1.at[units], sum_send_sem.at[g, 1])
+            await_bytes(from_plane.at[g, pl.ds(0, 15)], sum_send_sem.at[g, 2])
+            await_bytes(from_plane.at[g, pl.ds(0, 15)], sum_send_sem.at[g, 3])
+            await_bytes(from_1.at[units], sum_send_sem.at[g, 4])
+        else:
+            for level in (1, 2):
+                await_bytes(from_chips.at[pl.ds(0, CHIPS - 1)], sum_send_sem.at[g, level])
 
     for g in range(GROUPS):
         cols = slice(g * LANES, (g + 1) * LANES)
@@ -401,6 +463,8 @@
         d_scaled = (d_block.astype(F32) * inverse).astype(BF16)
         d_values = dot_cols(weights[g], d_scaled).astype(BF16)
         d_keyvals[:, width + g * LANES:width + (g + 1) * LANES] = d_values
+        if g > 0:
+            sum_1(g - 1)
         for c in range(9):
             part = slice(c * BLOCK, (c + 1) * BLOCK)
             d = dot(values[part, cols], d_block)
@@ -414,29 +478,46 @@
         both = dot(halo_t[...], jnp.concatenate([d_keys, d_values], axis=1)).astype(BF16)
         grads[4 * g + 1] = both[:, :LANES]
         grads[4 * g + 2] = both[:, LANES:]
-        advance(*range(g + 1))
-
-    for c, place in around(lat, lon):
-        parts[block_rows(c), :] = dot_cols(
-            d_keyvals[block_rows(c), :], w_qkv_ref[:, width:]
-        ).astype(BF16)
-        n = c - 1 if c > OWN else c
-        send_to(
-            parts.at[block_rows(c)], from_around.at[block_rows(n)],
-            parts_send_sem, parts_recv_sem, place,
-        )
-    advance(0, 1, 2, 3)
-    d_normed = dot_cols(d_keyvals[block_rows(OWN), :], w_qkv_ref[:, width:]) + dot_cols(
-        turned(d_query_t[...]), w_qkv_ref[:, :width]
-    )
+        sum_core(g)
+    sum_plane(0)
+
+    def node_part(c):
+        return dot_cols(d_keyvals[block_rows(c), :], w_qkv_ref[:, width:])
+
+    for lat_step in (-1, 1, 0):
+        for n, (sign, place) in enumerate(beside(lat, lon)):
+            slot_rows = pl.ds((2 * (lat_step % 3) + n) * BLOCK, BLOCK)
+            parts[slot_rows, :] = node_part(cell(lat_step, sign)).astype(BF16)
+            send_to(
+                parts.at[slot_rows], from_around.at[slot_rows],
+                parts_send_sem.at[lat_step % 3], parts_recv_sem.at[lat_step % 3], place,
+            )
+    scatter(3)
+    sum_plane(1)
+    d_normed = node_part(OWN) + dot_cols(turned(d_query_t[...]), w_qkv_ref[:, :width])
     mixed_ref[...] = (latent_ref[...] + dot_rows(attended_t[...], w_out_ref[...])).astype(BF16)
-    advance(0, 1, 2, 3)
     latent = latent_ref[...]
     centered = latent - jnp.mean(latent, axis=1, keepdims=True)
     inverse_std = lax.rsqrt(jnp.mean(centered * centered, axis=1, keepdims=True) + EPS)
     normalized = centered * inverse_std
-    await_bytes(from_around, parts_recv_sem)
-    for n in range(8):
+    sum_plane(2)
+    for n, (sign, place) in enumerate(above(lat, lon)):
+        at = sign % 3
+        part = node_part(cell(sign, 0))
+        arrived = from_around.at[pl.ds(2 * at * BLOCK, 2 * BLOCK)]
+        await_bytes(arrived, parts_recv_sem.at[at])
+        part = part + arrived[:BLOCK, :].astype(F32) + arrived[BLOCK:, :].astype(F32)
+        slot_rows = pl.ds((6 + n) * BLOCK, BLOCK)
+        parts[slot_rows, :] = part.astype(BF16)
+        send_to(
+            parts.at[slot_rows], from_around.at[slot_rows], parts_send_sem.at[3], parts_recv_sem.at[3], place
+        )
+    for g in range(3):
+        back_plane(g)
+    gather(3)
+    await_bytes(from_around.at[pl.ds(0, 2 * BLOCK)], parts_recv_sem.at[0])
+    await_bytes(from_around.at[pl.ds(6 * BLOCK, 2 * BLOCK)], parts_recv_sem.at[3])
+    for n in (0, 1, 6, 7):
         d_normed = d_normed + from_around[block_rows(n), :].astype(F32)
     scaled = d_normed * gain_ref[...]
     d_latent = cot.astype(F32) + inverse_std * (
@@ -448,7 +529,10 @@
     stacked = jnp.concatenate([node_grad[:, :half], node_grad[:, half:]], axis=0)
 
     await_bytes(send.at[pl.ds(0, (DEVICES - 1) * 2 * CAP)], send_sem)
-    for step in (0, 1, 7, 2, 6, 3, 5, 4):
+    for turn, step in enumerate((0, 1, 7, 2, 6, 3, 5, 4)):
+        if turn == 2:
+            for g in range(3):
+                back_1(g)
         to_lat = (lat + step) % LAT
         rows = tile_rows(to_lat, 2 * CAP * LON)
         send[rows, :] = dot(spread_ref[rows, :], stacked).astype(BF16)
@@ -466,11 +550,16 @@
     pltpu.make_async_copy(
         send.at[tile_rows(me, 2 * CAP)], returned_ref.at[tile_rows(me, 2 * CAP)], back_recv_sem
     ).start()
-    while min(reached) < len(stages):
-        advance(0, 1, 2, 3)
+    gather_core(3)
+    for g in range(3):
+        back_core(g)
+    for g in range(GROUPS):
+        sum_end(g)
     await_bytes(ids_send.at[pl.ds(0, DEVICES - 1)], ids_send_sem)
-    await_bytes(halo.at[pl.ds(0, 8 * BLOCK)], halo_send_sem)
-    await_bytes(from_around, parts_send_sem)
+    for n, blocks in enumerate((1, 1, 6)):
+        await_bytes(halo.at[pl.ds(0, blocks * BLOCK)], halo_send_sem.at[n])
+    for n in range(4):
+        await_bytes(parts.at[pl.ds(0, 2 * BLOCK)], parts_send_sem.at[n])
     await_bytes(send.at[pl.ds(0, (DEVICES - 1) * 2 * CAP)], back_send_sem)
     await_bytes(returned_ref, back_recv_sem)
 
@@ -480,7 +569,7 @@
     nodes = embed.shape[0]
     lanes = 2 * DEVICES * CAP
     pool = 9 * nodes
-    units = 4 * GROUPS
+    units, early = 4 * GROUPS, 4 * len(FIRST_AXES)
     vmem, dma = pltpu.VMEM, pltpu.SemaphoreType.DMA
     return pl.pallas_call(
         sublayer_kernel,
@@ -520,14 +609,14 @@
             vmem((units, width, LANES), BF16),
             vmem((units, ROWS_CORE, LANES), BF16),
             vmem((units, ROWS_CORE, LANES), BF16),
-            vmem((units, 3 * ROWS_1, LANES), BF16),
-            vmem((units, ROWS_1, LANES), BF16),
-            vmem((units, 3 * ROWS_2, LANES), BF16),
-            vmem((units, 4 * ROWS_2, LANES), BF16),
-            vmem((pool, width), BF16),
+            vmem((early, 3 * ROWS_1, LANES), BF16),
+            vmem((early, ROWS_1, LANES), BF16),
+            vmem((len(FIRST_AXES), 16, ROWS_2, LANES), BF16),
+            vmem((CHIPS, ROWS_2, LANES), BF16),
+            vmem((8 * nodes, width), BF16),
             vmem((8 * nodes, width), BF16),
             dma((4,)),
-        ] + [dma] * 6 + [dma((GROUPS, 7))] * 2 + [dma] * 4,
+        ] + [dma] * 4 + [dma((3,))] * 2 + [dma((GROUPS, 6))] * 2 + [dma((4,))] * 2 + [dma] * 2,
         compiler_params=pltpu.CompilerParams(
             collective_id=0, has_side_effects=True, vmem_limit_bytes=VMEM_LIMIT
         ),

time: 119 us -> 108 us (0.908)
  Pallas kernels: 118 us -> 107 us
    pallas_call x1, Pallas kernels: 112 us -> 102 us  [sublayer(): pl.pallas_call(sublayer_kernel, name='sublayer', out_shape=(jax.ShapeDtyp...]
where the time goes in v3:
time: 108 us
  Pallas kernels  107 us (99%)
    pallas_call x1, Pallas kernels, sublayer(): pl.pallas_call(sublayer_kernel, name='sublayer', out_shape=(jax.ShapeDtyp...  102 us
    pallas_call x1, Pallas kernels, finish(): pl.pallas_call(finish_kernel, name='finish', out_shape=(jax.ShapeDtypeStr...  5.69 us

profile of v3, /device:TPU:1, one launch (start us, length us, event | category | flops | bytes accessed | tf_op | source)
XLA Modules:
  0.0 107.9 jit_solution(12819260957137844921)
XLA Ops:
  0.6 101.6 %sublayer.1 = (bf16[128,512]{1,0:T(8,128)(2,1)}, bf16[16,512,128]{2,1,0:T(8,128)(2,1)}, bf16[2048,256]{1,0:T(8,128)(2,1)}, s32[512,128]{1,0:T(8,128)}) custom-call(bf16[512,512]{1,0:T(8,128)(2,1)} %grid_ref.1, s32[1,512]{1,0:T(1,128)} %bitcast.6, s32[1,512]{1,0:T(1,128)} %bitcast.7, s32[1,16]{1,0:T(1,128)} %listed_ref.1, f32[1,512]{1,0:T(1,128)} %bitcast.4, ...), custom_call_target="tpu_custom_call" | custom-call | tf_op jit(solution)/shard_map/sublayer/pallas_call | solution.py:574
  102.2 5.7 %finish.1 = (bf16[128,512]{1,0:T(8,128)(2,1)}, bf16[512,512]{1,0:T(8,128)(2,1)}, f32[512,1536]{1,0:T(8,128)}, f32[512,512]{1,0:T(8,128)}, f32[1,512]{1,0:T(1,128)}) custom-call(bf16[16,512,128]{2,1,0:T(8,128)(2,1)} %get-tuple-element.14.reduced_ref, bf16[2048,256]{1,0:T(8,128)(2,1)} %get-tuple-element.15.returned_ref, ...), custom_call_target="tpu_custom_call" | custom-call | tf_op jit(solution)/shard_map/finish/pallas_call | solution.py:656

commit v4 on v3

--- a/solution.py
+++ b/solution.py
@@ -124,14 +124,14 @@
 
 
 def sublayer_kernel(
-    grid_ref, owner_ref, node_ref, listed_ref, gain_ref, embed_hbm, w_qkv_hbm, w_out_hbm, cot_hbm,
-    mixed_ref, reduced_ref, returned_ref, flat_ref,
-    embed_ref, w_qkv_ref, w_out_ref, cot_ref,
+    owner_ref, node_ref, listed_ref, gain_ref, grid_hbm, embed_hbm, w_qkv_hbm, w_out_hbm, cot_hbm,
+    mixed_out, reduced_out, returned_ref, flat_out,
+    mixed_ref, reduced_ref, flat_ref, grid_ref, embed_ref, w_qkv_ref, w_out_ref, cot_ref,
     send, recv, ids_send, ids_recv,
     halo, halo_t, latent_ref, spread_ref, keys, values, q_blocks, d_blocks,
-    scores, weights, inverses, deltas, d_keyvals, attended_t, d_query_t,
+    scores, tops, weights, inverses, deltas, d_keyvals, attended_t, d_query_t,
     grads, from_core, held_0, from_1, held_1, from_plane, from_chips, parts, from_around,
-    load_sem, send_sem, recv_sem, ids_send_sem, ids_recv_sem, halo_send_sem, halo_recv_sem,
+    load_sem, store_sem, send_sem, recv_sem, ids_send_sem, ids_recv_sem, halo_send_sem, halo_recv_sem,
     sum_send_sem, sum_recv_sem, parts_send_sem, parts_recv_sem, back_send_sem, back_recv_sem,
 ):
     lat, lon = lax.axis_index("lat"), lax.axis_index("lon")
@@ -149,7 +149,7 @@
     loads = [
         pltpu.make_async_copy(src, dst, load_sem.at[i])
         for i, (src, dst) in enumerate(
-            ((embed_hbm, embed_ref), (w_qkv_hbm, w_qkv_ref), (w_out_hbm, w_out_ref), (cot_hbm, cot_ref))
+            ((grid_hbm, grid_ref), (embed_hbm, embed_ref), (w_qkv_hbm, w_qkv_ref), (w_out_hbm, w_out_ref), (cot_hbm, cot_ref))
         )
     ]
     for load in loads:
@@ -167,33 +167,32 @@
     flat = owner * CAP + slot
     named = (picked * (node_ref[...] + 1).astype(F32)).astype(BF16)
     ids_send[:, 0, :] = dot_cols(named, one_hot(iota((LANES, count), 0) == slot))
+    loads[0].wait()
     grid = grid_ref[...]
 
-    pl.semaphore_wait(barrier, DEVICES - 1)
-    for step in (0, 1, 7, 2, 6, 3, 5, 4):
-        to_lat = (lat + step) % LAT
-        chosen = one_hot(iota((LON * CAP, count), 0) + to_lat * (LON * CAP) == flat)
+    for k in range(LAT):
+        chosen = one_hot(iota((LON * CAP, count), 0) + k * (LON * CAP) == flat)
         block = dot(chosen, grid).reshape(LON, CAP, width)
         block = jnp.concatenate([block[:, :, :half], block[:, :, half:]], axis=1)
-        send[tile_rows(to_lat, 2 * CAP * LON), :] = block.reshape(2 * CAP * LON, half).astype(BF16)
-
-        def push(j, carry, to_lat=to_lat):
-            to_lon = (lon + j) % LON
-            other = to_lat * LON + to_lon
-            send_to(ids_send.at[other], ids_recv.at[me], ids_send_sem, ids_recv_sem, (to_lat, to_lon))
-            send_to(
-                send.at[tile_rows(other, 2 * CAP)], recv.at[tile_rows(me, 2 * CAP)],
-                send_sem, recv_sem, (to_lat, to_lon),
-            )
-            return carry
-
-        lax.fori_loop(1 if step == 0 else 0, LON, push, 0)
+        send[pl.ds(k * 2 * CAP * LON, 2 * CAP * LON), :] = block.reshape(2 * CAP * LON, half).astype(BF16)
+    pl.semaphore_wait(barrier, DEVICES - 1)
+
+    def push(step, carry):
+        other = (me + 53 * step) % DEVICES
+        place = (other // LON, other % LON)
+        send_to(ids_send.at[other], ids_recv.at[me], ids_send_sem, ids_recv_sem, place)
+        send_to(
+            send.at[tile_rows(other, 2 * CAP)], recv.at[tile_rows(me, 2 * CAP)], send_sem, recv_sem, place
+        )
+        return carry
+
+    lax.fori_loop(1, DEVICES, push, 0)
     pltpu.make_async_copy(ids_send.at[me], ids_recv.at[me], ids_recv_sem).start()
     pltpu.make_async_copy(
         send.at[tile_rows(me, 2 * CAP)], recv.at[tile_rows(me, 2 * CAP)], recv_sem
     ).start()
 
-    for load in loads:
+    for load in loads[1:]:
         load.wait()
     cot = cot_ref[...]
     d_t = turned(dot_cols(cot, w_out_ref[...]).astype(BF16))
@@ -247,44 +246,46 @@
     own_t = turned(own)
     blocks_of(q_blocks, turned(dot(own, w_qkv_ref[:, :width]).astype(BF16)))
 
-    def project(rows):
-        keys[rows, :] = dot(halo[rows, :], w_qkv_ref[:, width:2 * width]).astype(BF16)
-        values[rows, :] = dot(halo[rows, :], w_qkv_ref[:, 2 * width:]).astype(BF16)
-
+    def take(c):
+        rows = block_rows(c)
+        block = halo[rows, :]
+        keys[rows, :] = dot(block, w_qkv_ref[:, width:2 * width]).astype(BF16)
+        values[rows, :] = dot(block, w_qkv_ref[:, 2 * width:]).astype(BF16)
+        halo_t[:, rows] = turned(block)
+        for g in range(GROUPS):
+            s = dot(keys[rows, g * LANES:(g + 1) * LANES], q_blocks[g])
+            scores[g, rows, :] = s
+            tops[g, c:c + 1, :] = jnp.max(s, axis=0, keepdims=True) * (SCALE * TO_LOG2) + bias[c:c + 1, :]
+
+    take(OWN)
     for n, (step, _) in enumerate(above(lat, lon)):
         block = halo.at[block_rows(cell(-step, 0))]
         await_bytes(block, halo_recv_sem.at[n])
         for sign, place in beside(lat, lon):
             send_to(
                 block, halo.at[block_rows(cell(-step, -sign))],
-                halo_send_sem.at[2], halo_recv_sem.at[2], place,
+                halo_send_sem.at[3], halo_recv_sem.at[3], place,
             )
-    project(slice(OWN * BLOCK, (OWN + 1) * BLOCK))
+    await_bytes(halo.at[pl.ds(0, 2 * BLOCK)], halo_recv_sem.at[2])
+    for c in (1, 3, 5, 7):
+        take(c)
     codes = dot(one_hot(iota((lanes, DEVICES), 1) == (iota((lanes, DEVICES), 0) >> 4)), ids.astype(BF16))
     mine = (iota((lanes, LANES), 0) & 7) == iota((lanes, LANES), 1)
     code = jnp.sum(jnp.where(mine, codes, 0.0), axis=1, keepdims=True).astype(jnp.int32)
     code = jnp.where(code > 0, code - 1 + nodes * ((iota((lanes, 1), 0) >> 3) & 1), -1)
     spread_ref[...] = one_hot(iota((lanes, 2 * nodes), 1) == code)
 
-    await_bytes(halo.at[pl.ds(0, 6 * BLOCK)], halo_recv_sem.at[2])
-    project(slice(0, OWN * BLOCK))
-    project(slice((OWN + 1) * BLOCK, 9 * BLOCK))
-    halo_t[...] = turned(halo[...])
+    await_bytes(halo.at[pl.ds(0, 4 * BLOCK)], halo_recv_sem.at[3])
+    for c in (0, 2, 6, 8):
+        take(c)
 
     def forward(g, carry):
-        cols = pl.ds(pl.multiple_of(g * LANES, LANES), LANES)
-        q_block = q_blocks[g]
-        highest = None
-        for c in range(9):
-            part = slice(c * BLOCK, (c + 1) * BLOCK)
-            s = dot(keys[part, cols], q_block)
-            scores[part, :] = s
-            top = jnp.max(s, axis=0, keepdims=True) * (SCALE * TO_LOG2) + bias[c:c + 1, :]
-            highest = top if c == 0 else jnp.maximum(highest, top)
+        cols = slice(g * LANES, (g + 1) * LANES)
+        highest = jnp.max(tops[g, 0:9, :], axis=0, keepdims=True)
         total = jnp.zeros((1, COLUMNS), F32)
         for c in range(9):
             part = slice(c * BLOCK, (c + 1) * BLOCK)
-            w = jnp.exp2(scores[part, :] * (SCALE * TO_LOG2) - (highest - bias[c:c + 1, :]))
+            w = jnp.exp2(scores[g, part, :] * (SCALE * TO_LOG2) - (highest - bias[c:c + 1, :]))
             total = total + jnp.sum(w, axis=0, keepdims=True)
             weights[g, part, :] = w.astype(BF16)
         inverse = 1.0 / total
@@ -302,7 +303,8 @@
         deltas[g] = jnp.broadcast_to(delta, (8, COLUMNS))
         return carry
 
-    lax.fori_loop(0, GROUPS, forward, 0)
+    for g in range(GROUPS):
+        forward(g, 0)
     grad_w_out = dot(attended_t[...], cot).astype(BF16)
     for g in range(GROUPS):
         grads[4 * g + 3] = grad_w_out[:, g * LANES:(g + 1) * LANES]
@@ -455,6 +457,15 @@
         else:
             for level in (1, 2):
                 await_bytes(from_chips.at[pl.ds(0, CHIPS - 1)], sum_send_sem.at[g, level])
+
+    def weight_grads(g):
+        cols = slice(g * LANES, (g + 1) * LANES)
+        v_cols = slice(width + g * LANES, width + (g + 1) * LANES)
+        grads[4 * g] = dot_cols(own_t, d_query_t[cols, :]).astype(BF16)
+        both = jnp.concatenate([d_keyvals[:, cols], d_keyvals[:, v_cols]], axis=1)
+        both = dot(halo_t[...], both).astype(BF16)
+        grads[4 * g + 1] = both[:, :LANES]
+        grads[4 * g + 2] = both[:, LANES:]
 
     for g in range(GROUPS):
         cols = slice(g * LANES, (g + 1) * LANES)
@@ -474,12 +485,9 @@
         d_keyvals[:, cols] = d_keys
         d_query = (diagonal(dot_rows(keys[:, cols], weights[g])) * spread_heads(back)).astype(BF16)
         d_query_t[cols, :] = d_query
-        grads[4 * g] = dot_cols(own_t, d_query).astype(BF16)
-        both = dot(halo_t[...], jnp.concatenate([d_keys, d_values], axis=1)).astype(BF16)
-        grads[4 * g + 1] = both[:, :LANES]
-        grads[4 * g + 2] = both[:, LANES:]
-        sum_core(g)
-    sum_plane(0)
+        if g < GROUPS - 1:
+            weight_grads(g)
+            sum_core(g)
 
     def node_part(c):
         return dot_cols(d_keyvals[block_rows(c), :], w_qkv_ref[:, width:])
@@ -492,8 +500,11 @@
                 parts.at[slot_rows], from_around.at[slot_rows],
                 parts_send_sem.at[lat_step % 3], parts_recv_sem.at[lat_step % 3], place,
             )
+    weight_grads(3)
+    sum_core(3)
+    sum_plane(0)
+    sum_plane(1)
     scatter(3)
-    sum_plane(1)
     d_normed = node_part(OWN) + dot_cols(turned(d_query_t[...]), w_qkv_ref[:, :width])
     mixed_ref[...] = (latent_ref[...] + dot_rows(attended_t[...], w_out_ref[...])).astype(BF16)
     latent = latent_ref[...]
@@ -553,14 +564,26 @@
     gather_core(3)
     for g in range(3):
         back_core(g)
+    stores = [
+        pltpu.make_async_copy(mixed_ref, mixed_out, store_sem.at[0]),
+        pltpu.make_async_copy(flat_ref, flat_out, store_sem.at[1]),
+    ]
     for g in range(GROUPS):
         sum_end(g)
+        units = group_units(g)
+        stores.append(
+            pltpu.make_async_copy(reduced_ref.at[units], reduced_out.at[units], store_sem.at[2 + g])
+        )
+    for store in stores:
+        store.start()
     await_bytes(ids_send.at[pl.ds(0, DEVICES - 1)], ids_send_sem)
-    for n, blocks in enumerate((1, 1, 6)):
+    for n, blocks in enumerate((1, 1, 2, 4)):
         await_bytes(halo.at[pl.ds(0, blocks * BLOCK)], halo_send_sem.at[n])
     for n in range(4):
         await_bytes(parts.at[pl.ds(0, 2 * BLOCK)], parts_send_sem.at[n])
     await_bytes(send.at[pl.ds(0, (DEVICES - 1) * 2 * CAP)], back_send_sem)
+    for store in stores:
+        store.wait()
     await_bytes(returned_ref, back_recv_sem)
 
 
@@ -580,9 +603,13 @@
             jax.ShapeDtypeStruct((lanes, width // 2), BF16),
             jax.ShapeDtypeStruct((count, LANES), jnp.int32),
         ),
-        in_specs=[pl.BlockSpec(memory_space=vmem)] * 5 + [pl.BlockSpec(memory_space=pl.ANY)] * 4,
-        out_specs=[pl.BlockSpec(memory_space=vmem)] * 4,
+        in_specs=[pl.BlockSpec(memory_space=vmem)] * 4 + [pl.BlockSpec(memory_space=pl.ANY)] * 5,
+        out_specs=[pl.BlockSpec(memory_space=vmem if i == 2 else pl.ANY) for i in range(4)],
         scratch_shapes=[
+            vmem((nodes, width), BF16),
+            vmem((units, width, LANES), BF16),
+            vmem((count, LANES), jnp.int32),
+            vmem((count, width), BF16),
             vmem((nodes, width), BF16),
             vmem(w_qkv.shape, BF16),
             vmem(w_out.shape, BF16),
@@ -599,7 +626,8 @@
             vmem((pool, width), BF16),
             vmem((GROUPS, LANES, COLUMNS), BF16),
             vmem((GROUPS, LANES, COLUMNS), BF16),
-            vmem((pool, COLUMNS), F32),
+            vmem((GROUPS, pool, COLUMNS), F32),
+            vmem((GROUPS, 16, COLUMNS), F32),
             vmem((GROUPS, pool, COLUMNS), BF16),
             vmem((GROUPS, 8, COLUMNS), F32),
             vmem((GROUPS, 8, COLUMNS), F32),
@@ -615,14 +643,15 @@
             vmem((CHIPS, ROWS_2, LANES), BF16),
             vmem((8 * nodes, width), BF16),
             vmem((8 * nodes, width), BF16),
-            dma((4,)),
-        ] + [dma] * 4 + [dma((3,))] * 2 + [dma((GROUPS, 6))] * 2 + [dma((4,))] * 2 + [dma] * 2,
+            dma((5,)),
+            dma((2 + GROUPS,)),
+        ] + [dma] * 4 + [dma((4,))] * 2 + [dma((GROUPS, 6))] * 2 + [dma((4,))] * 2 + [dma] * 2,
         compiler_params=pltpu.CompilerParams(
             collective_id=0, has_side_effects=True, vmem_limit_bytes=VMEM_LIMIT
         ),
     )(
-        grid_rows, owner.reshape(1, count), node.reshape(1, count), listed, gain.reshape(1, width),
-        embed, w_qkv, w_out, cotangent,
+        owner.reshape(1, count), node.reshape(1, count), listed, gain.reshape(1, width),
+        grid_rows, embed, w_qkv, w_out, cotangent,
     )
 
 

time: 108 us -> 102 us (0.944)
  Pallas kernels: 107 us -> 101 us
    pallas_call x1, Pallas kernels: 102 us -> 95.1 us  [sublayer(): pl.pallas_call(sublayer_kernel, name='sublayer', out_shape=(jax.ShapeDtyp...]
where the time goes in v4:
time: 102 us; the launch traced here: 101 us
  Pallas kernels  101 us (99%)
    pallas_call x1, Pallas kernels, sublayer(): pl.pallas_call(sublayer_kernel, name='sublayer', out_shape=(jax.ShapeDtyp...  95.1 us
    pallas_call x1, Pallas kernels, finish(): pl.pallas_call(finish_kernel, name='finish', out_shape=(jax.ShapeDtypeStr...  5.69 us

profile of v4, /device:TPU:1, one launch (start us, length us, event | category | flops | bytes accessed | tf_op | source)
XLA Modules:
  0.0 101.5 jit_solution(1816251234996669103)
XLA Ops:
  0.6 95.1 %sublayer.1 = (bf16[128,512]{1,0:T(8,128)(2,1)}, bf16[16,512,128]{2,1,0:T(8,128)(2,1)}, bf16[2048,256]{1,0:T(8,128)(2,1)}, s32[512,128]{1,0:T(8,128)}) custom-call(s32[1,512]{1,0:T(1,128)} %bitcast.6, s32[1,512]{1,0:T(1,128)} %bitcast.7, s32[1,16]{1,0:T(1,128)} %listed_ref.1, f32[1,512]{1,0:T(1,128)} %bitcast.4, bf16[512,512]{1,0:T(8,128)(2,1)} %grid_hbm.1, ...), custom_call_target="tpu_custom_call" | custom-call | tf_op jit(solution)/shard_map/sublayer/pallas_call | solution.py:597
  95.8 5.7 %finish.1 = (bf16[128,512]{1,0:T(8,128)(2,1)}, bf16[512,512]{1,0:T(8,128)(2,1)}, f32[512,1536]{1,0:T(8,128)}, f32[512,512]{1,0:T(8,128)}, f32[1,512]{1,0:T(1,128)}) custom-call(bf16[16,512,128]{2,1,0:T(8,128)(2,1)} %get-tuple-element.14.reduced_ref, bf16[2048,256]{1,0:T(8,128)(2,1)} %get-tuple-element.15.returned_ref, ...), custom_call_target="tpu_custom_call" | custom-call | tf_op jit(solution)/shard_map/finish/pallas_call | solution.py:685

commit v5 on v4

--- a/solution.py
+++ b/solution.py
@@ -540,24 +540,20 @@
     stacked = jnp.concatenate([node_grad[:, :half], node_grad[:, half:]], axis=0)
 
     await_bytes(send.at[pl.ds(0, (DEVICES - 1) * 2 * CAP)], send_sem)
-    for turn, step in enumerate((0, 1, 7, 2, 6, 3, 5, 4)):
-        if turn == 2:
-            for g in range(3):
-                back_1(g)
-        to_lat = (lat + step) % LAT
-        rows = tile_rows(to_lat, 2 * CAP * LON)
-        send[rows, :] = dot(spread_ref[rows, :], stacked).astype(BF16)
-
-        def push_back(j, carry, to_lat=to_lat):
-            to_lon = (lon + j) % LON
-            other = to_lat * LON + to_lon
-            send_to(
-                send.at[tile_rows(other, 2 * CAP)], returned_ref.at[tile_rows(me, 2 * CAP)],
-                back_send_sem, back_recv_sem, (to_lat, to_lon),
-            )
-            return carry
-
-        lax.fori_loop(1 if step == 0 else 0, LON, push_back, 0)
+    send[...] = dot(spread_ref[...], stacked).astype(BF16)
+
+    def push_back(step, carry):
+        other = (me + 53 * step) % DEVICES
+        send_to(
+            send.at[tile_rows(other, 2 * CAP)], returned_ref.at[tile_rows(me, 2 * CAP)],
+            back_send_sem, back_recv_sem, (other // LON, other % LON),
+        )
+        return carry
+
+    lax.fori_loop(1, 64, push_back, 0)
+    for g in range(3):
+        back_1(g)
+    lax.fori_loop(64, DEVICES, push_back, 0)
     pltpu.make_async_copy(
         send.at[tile_rows(me, 2 * CAP)], returned_ref.at[tile_rows(me, 2 * CAP)], back_recv_sem
     ).start()

time: 102 us -> 101 us (level)
  no operation moved by 1% of the time
where the time goes in v5:
time: 101 us
  Pallas kernels  100 us (99%)
    pallas_call x1, Pallas kernels, sublayer(): pl.pallas_call(sublayer_kernel, name='sublayer', out_shape=(jax.ShapeDtyp...  94.5 us
    pallas_call x1, Pallas kernels, finish(): pl.pallas_call(finish_kernel, name='finish', out_shape=(jax.ShapeDtypeStr...  5.69 us

profile of v5, /device:TPU:1, one launch (start us, length us, event | category | flops | bytes accessed | tf_op | source)
XLA Modules:
  0.0 100.9 jit_solution(15954763975238631714)
XLA Ops:
  0.6 94.5 %sublayer.1 = (bf16[128,512]{1,0:T(8,128)(2,1)}, bf16[16,512,128]{2,1,0:T(8,128)(2,1)}, bf16[2048,256]{1,0:T(8,128)(2,1)}, s32[512,128]{1,0:T(8,128)}) custom-call(s32[1,512]{1,0:T(1,128)} %bitcast.6, s32[1,512]{1,0:T(1,128)} %bitcast.7, s32[1,16]{1,0:T(1,128)} %listed_ref.1, f32[1,512]{1,0:T(1,128)} %bitcast.4, bf16[512,512]{1,0:T(8,128)(2,1)} %grid_hbm.1, ...), custom_call_target="tpu_custom_call" | custom-call | tf_op jit(solution)/shard_map/sublayer/pallas_call | solution.py:593
  95.2 5.7 %finish.1 = (bf16[128,512]{1,0:T(8,128)(2,1)}, bf16[512,512]{1,0:T(8,128)(2,1)}, f32[512,1536]{1,0:T(8,128)}, f32[512,512]{1,0:T(8,128)}, f32[1,512]{1,0:T(1,128)}) custom-call(bf16[16,512,128]{2,1,0:T(8,128)(2,1)} %get-tuple-element.14.reduced_ref, bf16[2048,256]{1,0:T(8,128)(2,1)} %get-tuple-element.15.returned_ref, ...), custom_call_target="tpu_custom_call" | custom-call | tf_op jit(solution)/shard_map/finish/pallas_call | solution.py:681

commit v6 on v5

--- a/solution.py
+++ b/solution.py
@@ -128,7 +128,7 @@
     mixed_out, reduced_out, returned_ref, flat_out,
     mixed_ref, reduced_ref, flat_ref, grid_ref, embed_ref, w_qkv_ref, w_out_ref, cot_ref,
     send, recv, ids_send, ids_recv,
-    halo, halo_t, latent_ref, spread_ref, keys, values, q_blocks, d_blocks,
+    w_t, halo, halo_t, latent_ref, spread_ref, keys, values, q_blocks, d_blocks,
     scores, tops, weights, inverses, deltas, d_keyvals, attended_t, d_query_t,
     grads, from_core, held_0, from_1, held_1, from_plane, from_chips, parts, from_around,
     load_sem, store_sem, send_sem, recv_sem, ids_send_sem, ids_recv_sem, halo_send_sem, halo_recv_sem,
@@ -208,6 +208,8 @@
                 ]
 
     blocks_of(d_blocks, d_t)
+    for third in (1, 2):
+        w_t[(third - 1) * width:third * width, :] = turned(w_qkv_ref[:, third * width:(third + 1) * width])
     flat_ref[...] = jnp.broadcast_to(flat.astype(F32), (LANES, count)).T.astype(jnp.int32)
     listed = listed_ref[...]
     lat_step = listed // LON - lat
@@ -490,7 +492,7 @@
             sum_core(g)
 
     def node_part(c):
-        return dot_cols(d_keyvals[block_rows(c), :], w_qkv_ref[:, width:])
+        return dot(d_keyvals[block_rows(c), :], w_t[...])
 
     for lat_step in (-1, 1, 0):
         for n, (sign, place) in enumerate(beside(lat, lon)):
@@ -614,6 +616,7 @@
             vmem((lanes, width // 2), BF16),
             vmem((DEVICES, 1, LANES), F32),
             vmem((DEVICES, 1, LANES), F32),
+            vmem((2 * width, width), BF16),
             vmem((pool, width), BF16),
             vmem((width, pool), BF16),
             vmem((nodes, width), F32),

time: 101 us -> 101 us (level)
  no operation moved by 1% of the time
where the time goes in v6:
time: 101 us
  Pallas kernels  99.9 us (99%)
    pallas_call x1, Pallas kernels, sublayer(): pl.pallas_call(sublayer_kernel, name='sublayer', out_shape=(jax.ShapeDtyp...  94.2 us
    pallas_call x1, Pallas kernels, finish(): pl.pallas_call(finish_kernel, name='finish', out_shape=(jax.ShapeDtypeStr...  5.69 us

profile of v6, /device:TPU:1, one launch (start us, length us, event | category | flops | bytes accessed | tf_op | source)
XLA Modules:
  0.0 100.5 jit_solution(16466120510587341794)
XLA Ops:
  0.6 94.2 %sublayer.1 = (bf16[128,512]{1,0:T(8,128)(2,1)}, bf16[16,512,128]{2,1,0:T(8,128)(2,1)}, bf16[2048,256]{1,0:T(8,128)(2,1)}, s32[512,128]{1,0:T(8,128)}) custom-call(s32[1,512]{1,0:T(1,128)} %bitcast.6, s32[1,512]{1,0:T(1,128)} %bitcast.7, s32[1,16]{1,0:T(1,128)} %listed_ref.1, f32[1,512]{1,0:T(1,128)} %bitcast.4, bf16[512,512]{1,0:T(8,128)(2,1)} %grid_hbm.1, ...), custom_call_target="tpu_custom_call" | custom-call | tf_op jit(solution)/shard_map/sublayer/pallas_call | solution.py:595
  94.9 5.7 %finish.1 = (bf16[128,512]{1,0:T(8,128)(2,1)}, bf16[512,512]{1,0:T(8,128)(2,1)}, f32[512,1536]{1,0:T(8,128)}, f32[512,512]{1,0:T(8,128)}, f32[1,512]{1,0:T(1,128)}) custom-call(bf16[16,512,128]{2,1,0:T(8,128)(2,1)} %get-tuple-element.14.reduced_ref, bf16[2048,256]{1,0:T(8,128)(2,1)} %get-tuple-element.15.returned_ref, ...), custom_call_target="tpu_custom_call" | custom-call | tf_op jit(solution)/shard_map/finish/pallas_call | solution.py:684
